TPU v7x, 256 devices: a whole 4x4x8 slice. The times are simulated.
256 devices in a mesh: dp: 8 (over x, y_hi), dap: 32 (over y_lo, z, core).
Axes of the slice: x: 4, y: 4 (y_hi: 2, y_lo: 2; y = y_hi * 2 + y_lo), z: 8, core: 2. Of those that a mesh axis runs over, the one named last changes fastest.
Arguments:
- pair: bfloat16 [2048, 256, 128], P(('dp', 'dap')), parts along dimension 0, may hold values from -6 to 6
- gain_in: float32 [128], replicated, may hold values from 0.1 to 1.9
- w_proj: bfloat16 [128, 640], replicated, may hold values from -0.5 to 0.5
- gain_out: float32 [128], replicated, may hold values from 0.1 to 1.9
- w_out: bfloat16 [128, 128], replicated, may hold values from -0.5 to 0.5
- cotangent: bfloat16 [2048, 256, 128], P(('dp', 'dap')), parts along dimension 0, may hold values from -6 to 6
Outputs:
- update: bfloat16 [2048, 256, 128], P(('dp', 'dap')), parts along dimension 0
- grad_pair: bfloat16 [2048, 256, 128], P(('dp', 'dap')), parts along dimension 0
- grad_gain_in: float32 [1024], P('dp'), parts along dimension 0
- grad_w_proj: float32 [1024, 640], P('dp'), parts along dimension 0
- grad_gain_out: float32 [1024], P('dp'), parts along dimension 0
- grad_w_out: float32 [1024, 128], P('dp'), parts along dimension 0
There are 8 independent parts, one for each index of `dp`. A program takes and returns all parts, laid end to end along the dimension named above; an argument that names none is the same for every part. Nothing has to cross between parts.
All inputs are finite; a program needn't handle non-finite values.
Results may differ from a plain program's by a relative error of at most 0.035.
Values may be sent and summed in bfloat16 or wider, within the bound.
No kernel may reach another device: no remote copies, remote signals or barrier semaphores. Data moves between devices by JAX's collectives and lax.ppermute only.
A program may use at most 320 MiB of HBM per device.

v0:
```python
import jax
import jax.numpy as jnp
from jax import lax
from jax.sharding import PartitionSpec as P


def channel_norm(values):
    mean_val = jnp.mean(values, axis=-1, keepdims=True)
    shifted = values - mean_val
    variance = jnp.mean(shifted * shifted, axis=-1, keepdims=True)
    inv_std = lax.rsqrt(variance + 1e-05)
    return (shifted * inv_std, inv_std)


def norm_grad(scaled, centred, inv_std):
    first = jnp.mean(scaled, axis=-1, keepdims=True)
    second = jnp.mean(scaled * centred, axis=-1, keepdims=True)
    return inv_std * (scaled - first - centred * second)


def local(pair, gain_in, w_proj, gain_out, w_out, cotangent):
    width = gain_out.shape[0]
    centred, inv_std = channel_norm(pair.astype(jnp.float32))
    normed = (centred * gain_in).astype(jnp.bfloat16)
    projected = jnp.dot(normed, w_proj, preferred_element_type=jnp.float32)
    left_val = projected[..., 0:width]
    left_sig = jax.nn.sigmoid(projected[..., width : 2 * width])
    right_val = projected[..., 2 * width : 3 * width]
    right_sig = jax.nn.sigmoid(projected[..., 3 * width : 4 * width])
    out_gate = jax.nn.sigmoid(projected[..., 4 * width :])
    left_edge = (left_sig * left_val).astype(jnp.bfloat16)
    right_edge = (right_sig * right_val).astype(jnp.bfloat16)
    right_all = lax.all_gather(right_edge, "dap", axis=0, tiled=True)
    triangle = jnp.einsum("ikc,jkc->ijc", left_edge, right_all, preferred_element_type=jnp.float32)
    tri_centred, tri_inv_std = channel_norm(triangle)
    out_normed = (tri_centred * gain_out).astype(jnp.bfloat16)
    out_proj = jnp.dot(out_normed, w_out, preferred_element_type=jnp.float32)
    update = (out_gate * out_proj).astype(jnp.bfloat16)
    grad_upd = cotangent.astype(jnp.float32)
    grad_gate = grad_upd * out_proj
    grad_proj_out = (grad_upd * out_gate).astype(jnp.bfloat16)
    grad_w_out = jnp.einsum(
        "ijh,ijc->hc", out_normed, grad_proj_out, preferred_element_type=jnp.float32
    )
    grad_normed_out = jnp.einsum(
        "ijc,hc->ijh", grad_proj_out, w_out, preferred_element_type=jnp.float32
    )
    grad_gain_out = jnp.sum(grad_normed_out * tri_centred, axis=(0, 1))
    grad_triangle = norm_grad(grad_normed_out * gain_out, tri_centred, tri_inv_std).astype(
        jnp.bfloat16
    )
    grad_left = jnp.einsum(
        "ijc,jkc->ikc", grad_triangle, right_all, preferred_element_type=jnp.float32
    )
    grad_right = lax.psum_scatter(
        jnp.einsum(
            "ijc,ikc->jkc", grad_triangle, left_edge, preferred_element_type=jnp.float32
        ).astype(jnp.bfloat16),
        "dap",
        scatter_dimension=0,
        tiled=True,
    ).astype(jnp.float32)
    grad_projected = jnp.concatenate(
        [
            grad_left * left_sig,
            grad_left * left_val * left_sig * (1.0 - left_sig),
            grad_right * right_sig,
            grad_right * right_val * right_sig * (1.0 - right_sig),
            grad_gate * out_gate * (1.0 - out_gate),
        ],
        axis=-1,
    ).astype(jnp.bfloat16)
    grad_w_proj = jnp.einsum(
        "ijc,ijd->cd", normed, grad_projected, preferred_element_type=jnp.float32
    )
    grad_normed = jnp.einsum(
        "ijd,cd->ijc", grad_projected, w_proj, preferred_element_type=jnp.float32
    )
    grad_gain_in = jnp.sum(grad_normed * centred, axis=(0, 1))
    grad_pair = norm_grad(grad_normed * gain_in, centred, inv_std).astype(jnp.bfloat16)
    summed = (
        lax.psum(grad_gain_in.astype(jnp.bfloat16), "dap").astype(jnp.float32),
        lax.psum(grad_w_proj.astype(jnp.bfloat16), "dap").astype(jnp.float32),
        lax.psum(grad_gain_out.astype(jnp.bfloat16), "dap").astype(jnp.float32),
        lax.psum(grad_w_out.astype(jnp.bfloat16), "dap").astype(jnp.float32),
    )
    return (update, grad_pair, summed[0], summed[1], summed[2], summed[3])


def solution(mesh):
    in_specs = (P(("dp", "dap"), None, None), P(), P(), P(), P(), P(("dp", "dap"), None, None))
    out_specs = (
        P(("dp", "dap"), None, None),
        P(("dp", "dap"), None, None),
        P("dp"),
        P("dp", None),
        P("dp"),
        P("dp", None),
    )
    return jax.shard_map(local, mesh=mesh, in_specs=in_specs, out_specs=out_specs, check_vma=False)
```

profile of v0, /device:TPU:1, one launch (start us, length us, event | category | flops | bytes accessed | tf_op | source)
XLA Modules:
  0.0 655.6 jit_solution(3008698962499837829)
XLA Ops:
  7.2 0.0 copy-start
  7.2 0.0 all-gather.2.cloned.1.call-start
  7.2 1.3 copy.28
  8.5 0.1 convert_reduce_fusion
  8.6 0.2 fusion.14
  8.8 0.0 copy-done
  8.8 0.0 copy-start.2
  8.8 0.0 copy-start.6
  8.8 1.7 fusion.47
  10.5 0.0 copy-start.1
  10.5 2.4 copy-done.1
  12.9 1.3 multiply_convert_fusion.3
  14.2 0.0 all-gather.2.cloned.1.call-update
  14.2 0.0 reduce-scatter.2.cloned.1.call-start
  14.3 0.4 copy.31
  14.7 0.0 copy-done.2
  14.7 0.0 copy-done.6
  14.7 1.7 fusion.51
  16.4 101.9 %all-gather.2.cloned.1.call-done = bf16[256,256,128]{2,1,0:T(8,128)(2,1)} async-done(((bf16[8,256,128]{2,1,0:T(8,128)(2,1)}), bf16[256,256,128]{2,1,0:T(8,128)(2,1)}) %all-gather.2.cloned.1.call-update) | async-done | bytes 16777232 | tf_op jit(solution)/shard_map/all_gather | solution.py:33
  118.4 22.1 %copy.30 = bf16[256,256,128]{1,0,2:T(8,128)(2,1)} copy(bf16[256,256,128]{2,1,0:T(8,128)(2,1)} %all-gather.2.cloned.1.call-done) | data formatting | bytes 33554432 | tf_op jit(solution)/shard_map/all_gather | solution.py:33
  140.5 0.0 copy-start.5
  140.5 8.0 %fusion.58 = (f32[8,256]{1,0:T(8,128)S(1)}, f32[8,256,128]{1,0,2:T(8,128)S(1)}) fusion(bf16[256,256,128]{1,0,2:T(8,128)(2,1)} %copy.30, bf16[8,256,128]{1,0,2:T(8,128)(2,1)S(1)} %copy.31), kind=kOutput, calls=%fused_computation.86 | convolution fusion | flops 134477824 | bytes 18358272 | tf_op jit(solution)/shard_map/ikc,jkc->ijc/dot_general | solution.py:34
  148.5 0.2 multiply_reduce_fusion.2
  148.7 0.0 copy-done.5
  148.7 1.5 multiply_reduce_fusion
  150.2 1.5 multiply_convert_fusion
  151.7 8.1 %fusion.60 = bf16[128,256,256]{2,1,0:T(8,128)(2,1)} fusion(bf16[8,256,128]{1,0,2:T(8,128)(2,1)S(1)} %copy.31, bf16[8,256,128]{1,0,2:T(8,128)(2,1)S(1)} %get-tuple-element.29), kind=kOutput, calls=%fused_computation.88 | convolution fusion | flops 134217728 | bytes 17825792 | tf_op jit(solution)/shard_map/ijc,ikc->jkc/dot_general | solution.py:56
  159.8 24.3 %copy.39 = bf16[128,256,256]{0,1,2:T(8,128)(2,1)} copy(bf16[128,256,256]{2,1,0:T(8,128)(2,1)} %fusion.60) | data formatting | bytes 33554432 | tf_op jit(solution)/shard_map/ijc,ikc->jkc/dot_general | solution.py:56
  184.1 0.0 reduce-scatter.2.cloned.1.call-update
  184.1 0.2 all-reduce.3.cloned.1.call-start
  184.3 7.0 %fusion.59 = f32[128,256,8]{1,2,0:T(8,128)S(1)} fusion(bf16[256,256,128]{1,0,2:T(8,128)(2,1)} %copy.30, bf16[8,256,128]{1,0,2:T(8,128)(2,1)S(1)} %get-tuple-element.29), kind=kOutput, calls=%fused_computation.87 | convolution fusion | flops 134217728 | bytes 18350080 | tf_op jit(solution)/shard_map/ijc,jkc->ikc/dot_general | solution.py:52
  191.3 0.4 copy.37
  191.7 0.0 copy-start.3
  191.7 2.4 fusion.38
  194.2 2.6 multiply_convert_fusion.1
  196.8 0.0 copy-done.3
  196.8 1.7 fusion.7
  198.5 0.0 copy-start.4
  198.5 2.8 fusion.37
  201.3 123.3 %reduce-scatter.2.cloned.1.call-done = bf16[8,256,128]{2,1,0:T(8,128)(2,1)} async-done(((bf16[256,256,128]{2,1,0:T(8,128)(2,1)}), bf16[8,256,128]{2,1,0:T(8,128)(2,1)}) %reduce-scatter.2.cloned.1.call-update) | async-done | bytes 524304 | tf_op jit(solution)/shard_map/reduce_scatter | solution.py:55
  324.7 2.5 fusion.40
  327.2 2.9 fusion.39
  330.1 2.4 fusion.41
  332.5 0.0 copy-done.4
  332.5 3.0 fusion.6
  335.5 2.8 fusion.13
  338.4 105.2 %all-reduce = (bf16[128]{0:T(256)(128)(2,1)S(1)}, bf16[128]{0:T(256)(128)(2,1)S(1)}, bf16[128,128]{1,0:T(8,128)(2,1)S(1)}) all-reduce(bf16[128]{0:T(256)(128)(2,1)S(1)} %get-tuple-element.20, bf16[128]{0:T(256)(128)(2,1)S(1)} %get-tuple-element.18, bf16[128,128]{1,0:T(8,128)(2,1)S(1)} %fusion.7), channel_id=1, replica_groups=mesh['dp'=8,'dap'=32] {'dap'}, use_global_device_ids=true, to_apply=%region_10.0 | all-reduce | flops 16640 | bytes 66560 | tf_op jit(solution)/shard_map/psum | solution.py:82
  443.6 0.5 convert_element_type.78
  444.1 0.0 all-reduce.3.cloned.1.call-update
  444.1 0.5 convert_element_type.82
  444.7 0.3 fusion.12
  445.0 1.0 copy.43
  446.0 0.6 convert_element_type.84
  446.6 200.8 %all-reduce.3.cloned.1.call-done = bf16[128,640]{1,0:T(8,128)(2,1)} async-done(((bf16[128,640]{1,0:T(8,128)(2,1)}), bf16[128,640]{1,0:T(8,128)(2,1)}) %all-reduce.3.cloned.1.call-update) | async-done | bytes 163856 | tf_op jit(solution)/shard_map/psum | solution.py:83
  647.4 1.7 convert_element_type.80
  (7 shorter events, 0.0 us)
Async XLA Ops:
  7.2 1.6 copy-start
  7.2 111.2 %all-gather.2.cloned.1.call-start = ((), (), s32[]{:S(2)}) async-start(), calls=%async_computation.1 | async-start | bytes 17301504 | tf_op jit(solution)/shard_map/all_gather | solution.py:33
  8.8 5.9 copy-start.2
  8.8 5.9 copy-start.6
  10.5 2.4 copy-start.1
  14.2 310.4 %reduce-scatter.2.cloned.1.call-start = ((), (), s32[]{:S(2)}) async-start(), calls=%async_computation.2 | async-start | bytes 17301504 | tf_op jit(solution)/shard_map/reduce_scatter | solution.py:55
  140.5 8.2 %copy-start.5 = (f32[128]{0:T(128)S(1)}, f32[128]{0:T(128)}, u32[]{:S(2)}) copy-start(f32[128]{0:T(128)} %param.9) | copy-start | bytes 1540
  184.1 463.3 %all-reduce.3.cloned.1.call-start = ((), (), s32[]{:S(2)}) async-start(), calls=%async_computation.3 | async-start | bytes 327680 | tf_op jit(solution)/shard_map/psum | solution.py:83
  191.7 5.0 copy-start.3
  198.5 134.0 %copy-start.4 = (f32[128]{0:T(128)S(1)}, f32[128]{0:T(128)}, u32[]{:S(2)}) copy-start(f32[128]{0:T(128)} %param.7) | copy-start | bytes 1540
Sparse Core Ops, SparseCore 0:
  14.4 103.9 all-gather.1
  184.2 140.3 reduce-scatter.1
  444.3 203.1 all-reduce.2
where the time goes:
time: 657 us; the launch traced here: 656 us
  waiting for transfers between devices  426 us (65%)
  blocking collectives  105 us (16%)
  local copies, waits for them, and re-layouts  51.9 us (8%)
  matrix products  36.7 us (6%)
  other arithmetic  21.4 us (3%)
  between operations  13.9 us (2%)
    psum x1, waiting for transfers between devices, local(): lax.psum(grad_w_proj.astype(jnp.bfloat16), 'dap').astype(jnp.float32)  201 us
    reduce_scatter x1, waiting for transfers between devices, local(): lax.psum_scatter(jnp.einsum('ijc,ikc->jkc', grad_triangle, left_edge, pre...  123 us
    psum x1, blocking collectives, local(): lax.psum(grad_gain_in.astype(jnp.bfloat16), 'dap').astype(jnp.float32)  105 us
    all_gather x1, waiting for transfers between devices, local(): right_all = lax.all_gather(right_edge, 'dap', axis=0, tiled=True)  102 us
    dot_general x1, local copies, waits for them, and re-layouts, local(): jnp.einsum('ijc,ikc->jkc', grad_triangle, left_edge, preferred_element_ty...  24.3 us
    all_gather x1, local copies, waits for them, and re-layouts, local(): right_all = lax.all_gather(right_edge, 'dap', axis=0, tiled=True)  22.1 us
  transfers between devices with their start and end apart: 3, of which 3 were waited for; matrix products, arithmetic and copies ran while one was open for 3% of the time, Pallas kernels for 0%

commit v1 on v0

v1 whole, which is shorter than its diff:
```python
import jax
import jax.numpy as jnp
from jax import lax
from jax.sharding import PartitionSpec as P


def channel_norm(values):
    mean_val = jnp.mean(values, axis=-1, keepdims=True)
    shifted = values - mean_val
    variance = jnp.mean(shifted * shifted, axis=-1, keepdims=True)
    inv_std = lax.rsqrt(variance + 1e-05)
    return (shifted * inv_std, inv_std)


def norm_grad(scaled, centred, inv_std):
    first = jnp.mean(scaled, axis=-1, keepdims=True)
    second = jnp.mean(scaled * centred, axis=-1, keepdims=True)
    return inv_std * (scaled - first - centred * second)


def exchange(values):
    return lax.all_to_all(values, "dap", 0, 0, tiled=True)


def local(devices, pair, gain_in, w_proj, gain_out, w_out, cotangent):
    width = gain_out.shape[0]
    rows, res, _ = pair.shape
    share = width // devices
    f32, bf16 = jnp.float32, jnp.bfloat16

    def to_channels(values):
        sent = jnp.stack([v.astype(bf16) for v in values])
        sent = sent.reshape(len(values), rows, res, devices, share).transpose(3, 0, 4, 1, 2)
        got = exchange(sent)
        return got.transpose(1, 2, 0, 3, 4).reshape(len(values), share, devices * rows, res)

    def to_rows(values):
        sent = values.astype(bf16).reshape(-1, share, devices, rows, res).transpose(2, 0, 1, 3, 4)
        got = exchange(sent)
        return got.transpose(1, 3, 4, 0, 2).reshape(-1, rows, res, width)

    centred, inv_std = channel_norm(pair.astype(f32))
    normed = (centred * gain_in).astype(bf16)
    projected = jnp.dot(normed, w_proj, preferred_element_type=f32)
    left_val = projected[..., 0:width]
    left_sig = jax.nn.sigmoid(projected[..., width : 2 * width])
    right_val = projected[..., 2 * width : 3 * width]
    right_sig = jax.nn.sigmoid(projected[..., 3 * width : 4 * width])
    out_gate = jax.nn.sigmoid(projected[..., 4 * width :])
    edges = to_channels([left_sig * left_val, right_sig * right_val])
    left, right = edges[0], edges[1]
    triangle = jnp.einsum("cik,cjk->cij", left, right, preferred_element_type=f32)
    triangle = to_rows(triangle)[0].astype(f32)
    tri_centred, tri_inv_std = channel_norm(triangle)
    out_normed = (tri_centred * gain_out).astype(bf16)
    out_proj = jnp.dot(out_normed, w_out, preferred_element_type=f32)
    update = (out_gate * out_proj).astype(bf16)
    grad_upd = cotangent.astype(f32)
    grad_gate = grad_upd * out_proj
    grad_proj_out = (grad_upd * out_gate).astype(bf16)
    grad_w_out = jnp.einsum("ijh,ijc->hc", out_normed, grad_proj_out, preferred_element_type=f32)
    grad_normed_out = jnp.einsum("ijc,hc->ijh", grad_proj_out, w_out, preferred_element_type=f32)
    grad_gain_out = jnp.sum(grad_normed_out * tri_centred, axis=(0, 1))
    grad_triangle = norm_grad(grad_normed_out * gain_out, tri_centred, tri_inv_std)
    grad_tri = to_channels([grad_triangle])[0]
    grad_left = jnp.einsum("cij,cjk->cik", grad_tri, right, preferred_element_type=f32)
    grad_right = jnp.einsum("cij,cik->cjk", grad_tri, left, preferred_element_type=f32)
    grads = to_rows(jnp.stack([grad_left, grad_right])).astype(f32)
    grad_left, grad_right = grads[0], grads[1]
    grad_projected = jnp.concatenate(
        [
            grad_left * left_sig,
            grad_left * left_val * left_sig * (1.0 - left_sig),
            grad_right * right_sig,
            grad_right * right_val * right_sig * (1.0 - right_sig),
            grad_gate * out_gate * (1.0 - out_gate),
        ],
        axis=-1,
    ).astype(bf16)
    grad_w_proj = jnp.einsum("ijc,ijd->cd", normed, grad_projected, preferred_element_type=f32)
    grad_normed = jnp.einsum("ijd,cd->ijc", grad_projected, w_proj, preferred_element_type=f32)
    grad_gain_in = jnp.sum(grad_normed * centred, axis=(0, 1))
    grad_pair = norm_grad(grad_normed * gain_in, centred, inv_std).astype(bf16)

    blocks = [grad_w_proj[:, b * width : (b + 1) * width] for b in range(5)] + [grad_w_out]
    matrices = jnp.concatenate(blocks, axis=0).astype(bf16).reshape(devices, -1, width)
    gains = jnp.stack([grad_gain_in, grad_gain_out]).astype(bf16)
    gains = jnp.broadcast_to(gains[None], (devices, 2, width))
    got = exchange(jnp.concatenate([matrices, gains], axis=1)).astype(f32)
    total = jnp.sum(got, axis=0)
    gains = total[-2:]
    mine = total[:-2].astype(bf16)
    full = exchange(jnp.broadcast_to(mine[None], (devices,) + mine.shape))
    full = full.astype(f32).reshape(6, width, width)
    grad_w_proj = jnp.concatenate([full[b] for b in range(5)], axis=1)
    return (update, grad_pair, gains[0], grad_w_proj, gains[1], full[5])


def solution(mesh):
    devices = mesh.shape["dap"]

    def program(*args):
        return local(devices, *args)

    in_specs = (P(("dp", "dap"), None, None), P(), P(), P(), P(), P(("dp", "dap"), None, None))
    out_specs = (
        P(("dp", "dap"), None, None),
        P(("dp", "dap"), None, None),
        P("dp"),
        P("dp", None),
        P("dp"),
        P("dp", None),
    )
    return jax.shard_map(program, mesh=mesh, in_specs=in_specs, out_specs=out_specs, check_vma=False)
```

time: 657 us -> 189 us (0.29)
  waiting for transfers between devices: 426 us -> 43.8 us
  local copies, waits for them, and re-layouts: 51.9 us -> 15.3 us
  blocking collectives: 105 us -> 81.4 us
  matrix products: 36.7 us -> 13.3 us
  starting transfers between devices: 0.3 us -> 16.9 us
  between operations: 13.9 us -> 1.04 us
    psum x1 -> x0, waiting for transfers between devices: 201 us -> none  [local(): lax.psum(grad_w_proj.astype(jnp.bfloat16), 'dap').astype(jnp.float32)]
    reduce_scatter x1 -> x0, waiting for transfers between devices: 123 us -> none  [local(): lax.psum_scatter(jnp.einsum('ijc,ikc->jkc', grad_triangle, left_edge, pre...]
    psum x1 -> x0, blocking collectives: 105 us -> none  [local(): lax.psum(grad_gain_in.astype(jnp.bfloat16), 'dap').astype(jnp.float32)]
    all_gather x1 -> x0, waiting for transfers between devices: 102 us -> none  [local(): right_all = lax.all_gather(right_edge, 'dap', axis=0, tiled=True)]
    all_to_all x0 -> x3, blocking collectives: none -> 81.4 us  [exchange(): return lax.all_to_all(values, 'dap', 0, 0, tiled=True)]
    all_to_all x0 -> x3, waiting for transfers between devices: none -> 43.8 us  [exchange(): return lax.all_to_all(values, 'dap', 0, 0, tiled=True)]
    dot_general x2 -> x0, local copies, waits for them, and re-layouts: 24.7 us -> none  [the longest x1 24.3 us: local(): jnp.einsum('ijc,ikc->jkc', grad_triangle, left_edge, preferred_element_ty...]
    all_gather x1 -> x0, local copies, waits for them, and re-layouts: 22.1 us -> none  [local(): right_all = lax.all_gather(right_edge, 'dap', axis=0, tiled=True)]
where the time goes in v1:
time: 189 us; the launch traced here: 188 us
  blocking collectives  81.4 us (43%)
  waiting for transfers between devices  43.8 us (23%)
  starting transfers between devices  16.9 us (9%)
  other arithmetic  16.3 us (9%)
  local copies, waits for them, and re-layouts  15.3 us (8%)
  matrix products  13.3 us (7%)
    all_to_all x3, blocking collectives, exchange(): return lax.all_to_all(values, 'dap', 0, 0, tiled=True)  81.4 us
    all_to_all x3, waiting for transfers between devices, exchange(): return lax.all_to_all(values, 'dap', 0, 0, tiled=True)  43.8 us
    all_to_all x3, starting transfers between devices, exchange(): return lax.all_to_all(values, 'dap', 0, 0, tiled=True)  16.9 us
    unnamed x4, other arithmetic  8.63 us
    unnamed x33, local copies, waits for them, and re-layouts  6.38 us
  transfers between devices with their start and end apart: 3, of which 3 were waited for; matrix products, arithmetic and copies ran while one was open for 3% of the time, Pallas kernels for 0%

profile of v1, /device:TPU:1, one launch (start us, length us, event | category | flops | bytes accessed | tf_op | source)
XLA Modules:
  0.0 187.9 jit_solution(3216346522849513295)
XLA Ops:
  0.6 0.0 copy-start
  0.6 1.3 copy.46
  1.9 0.1 convert_reduce_fusion
  2.0 0.2 fusion.18
  2.2 1.6 fusion.54
  3.8 0.6 multiply_convert_fusion.8
  4.4 1.7 copy-done.1
  6.2 0.4 copy.48
  6.6 0.4 copy.49
  7.0 0.1 maximum_bitcast_fusion
  7.1 0.1 copy.50
  7.2 37.4 %all_to_all.30 = bf16[32,2,4,8,256]{4,3,2,1,0:T(8,128)(2,1)S(1)} all-to-all(bf16[32,2,4,8,256]{4,3,2,1,0:T(8,128)(2,1)S(1)} %copy.50), channel_id=1, replica_groups=mesh['dp'=8,'dap'=32] {'dap'}, dimensions={0} | all-to-all | bytes 2097152 | tf_op jit(solution)/shard_map/all_to_all | solution.py:22
  44.5 0.1 fusion.72
  44.6 0.3 fusion.6
  45.0 0.0 copy-start.3
  45.0 0.0 copy-start.9
  45.0 0.0 copy-start.10
  45.0 0.1 copy.122
  45.1 22.5 %all_to_all.31 = bf16[32,1,4,8,256]{4,3,2,1,0:T(8,128)(2,1)S(1)} all-to-all(bf16[32,1,4,8,256]{4,3,2,1,0:T(8,128)(2,1)S(1)} %bitcast.123), channel_id=1, replica_groups=mesh['dp'=8,'dap'=32] {'dap'}, dimensions={0} | all-to-all | bytes 1048576 | tf_op jit(solution)/shard_map/all_to_all | solution.py:22
  67.6 0.1 bitcast_reduce_fusion
  67.7 0.2 fusion.34
  67.9 0.1 convert_element_type.94
  68.0 0.0 copy-done.3
  68.1 0.0 copy-done.9
  68.1 0.0 copy-done.10
  68.1 2.2 %multiply_reduce_fusion = (bf16[128]{0:T(256)(128)(2,1)S(1)}, f32[8,256]{1,0:T(8,128)S(1)}, f32[8,256]{1,0:T(8,128)S(1)}, f32[8,256,128]{1,2,0:T(8,128)S(1)}) fusion(f32[8,256]{1,0:T(8,128)S(1)} %add_rsqrt_fusion, f32[8,256]{1,0:T(8,128)S(1)} %broadcast_multiply_fusion.4, f32[8,256,128]{1,0,2:T(8,128)S(1)} %bitcast.116, f32[128]{0:T(128)S(1)} %copy-done.9, ...), kind=kOutput, calls=%fused_computation.54 | convolution fusion | flops 70774656 | bytes 3736320 | tf_op jit(solution)/shard_map/ijc,hc->ijh/dot_general | solution.py:62
  70.3 1.3 multiply_convert_fusion.4
  71.6 1.2 reshape_stack.3
  72.7 0.3 copy.121
  73.0 21.5 %all_to_all.32 = bf16[32,1,4,8,256]{4,2,3,1,0:T(4,128)(2,1)S(1)} all-to-all(bf16[32,1,4,8,256]{4,2,3,1,0:T(4,128)(2,1)S(1)} %bitcast.124), channel_id=1, replica_groups=mesh['dp'=8,'dap'=32] {'dap'}, dimensions={0} | all-to-all | bytes 1048576 | tf_op jit(solution)/shard_map/all_to_all | solution.py:22
  94.5 0.3 fusion.7
  94.8 0.4 fusion.8
  95.2 1.2 copy_bitcast_fusion
  96.3 5.7 %all-to-all-start.3 = ((bf16[32,2,4,8,256]{4,3,2,1,0:T(8,128)(2,1)}), bf16[32,2,4,8,256]{4,3,2,1,0:T(8,128)(2,1)S(1)}, u32[]{:S(2)}, u32[]{:S(2)}) async-start(bf16[32,2,4,8,256]{4,3,2,1,0:T(8,128)(2,1)} %copy_bitcast_fusion), calls=%async_computation.3 | async-start | bytes 2097152 | tf_op jit(solution)/shard_map/all_to_all | solution.py:22
  102.0 3.0 %multiply_convert_fusion.5 = (bf16[8,256,128]{2,1,0:T(8,128)(2,1)}, f32[8,256,128]{2,1,0:T(8,128)}) fusion(f32[8,256,640]{2,1,0:T(8,128)} %copy-done.1, bf16[128,128]{1,0:T(8,128)(2,1)S(1)} %copy-done.10, f32[128]{0:T(128)S(1)} %copy-done.9, f32[8,256]{1,0:T(8,128)S(1)} %add_rsqrt_fusion, f32[8,256]{1,0:T(8,128)S(1)} %broadcast_multiply_fusion.4, ...), kind=kOutput, calls=%fused_computation.61 | convolution fusion | flops 69468160 | bytes 3719680 | tf_op jit(solution)/shard_map/dot_general | solution.py:56
  104.9 23.4 %all-to-all-done.3 = bf16[32,2,4,8,256]{4,3,2,1,0:T(8,128)(2,1)S(1)} async-done(((bf16[32,2,4,8,256]{4,3,2,1,0:T(8,128)(2,1)}), bf16[32,2,4,8,256]{4,3,2,1,0:T(8,128)(2,1)S(1)}, u32[]{:S(2)}, u32[]{:S(2)}) %all-to-all-start.3) | async-done | bytes 1048608 | tf_op jit(solution)/shard_map/all_to_all | solution.py:22
  128.4 0.3 convert_bitcast_fusion
  128.6 1.5 fusion.71
  130.1 1.6 copy.64
  131.7 1.5 fusion.35
  133.2 1.9 %fusion.36 = bf16[8,256,640]{2,1,0:T(8,128)(2,1)S(1)} fusion(bf16[8,256,640]{2,1,0:T(8,128)(2,1)S(1)} %fusion.35, f32[8,256,128]{2,1,0:T(8,128)S(1)} %copy.64, f32[8,256,640]{2,1,0:T(8,128)} %copy-done.1), kind=kLoop, calls=%fused_computation.68 | loop fusion | flops 2097152 | bytes 3670016
  135.2 1.5 copy-done.5
  136.7 1.6 copy.66
  138.3 0.0 copy-start.4
  138.3 2.4 %fusion.37 = bf16[8,256,640]{2,1,0:T(8,128)(2,1)} fusion(bf16[8,256,640]{2,1,0:T(8,128)(2,1)} %copy-done.5, f32[8,256,128]{2,1,0:T(8,128)S(1)} %copy.66, f32[8,256,640]{2,1,0:T(8,128)} %copy-done.1), kind=kLoop, calls=%fused_computation.69 | loop fusion | flops 1310720 | bytes 2621440
  140.7 2.7 %fusion.38 = bf16[8,256,640]{2,1,0:T(8,128)(2,1)} fusion(bf16[8,256,640]{2,1,0:T(8,128)(2,1)} %fusion.37, f32[8,256,128]{2,1,0:T(8,128)S(1)} %copy.66, f32[8,256,640]{2,1,0:T(8,128)} %copy-done.1), kind=kLoop, calls=%fused_computation.70 | loop fusion | flops 2097152 | bytes 3670016
  143.5 2.4 %fusion.39 = bf16[8,256,640]{2,1,0:T(8,128)(2,1)} fusion(bf16[8,256,640]{2,1,0:T(8,128)(2,1)} %fusion.38, f32[8,256,128]{2,1,0:T(8,128)S(1)} %copy-done.2, bf16[8,256,128]{2,1,0:T(8,128)(2,1)S(1)} %copy-done.4, f32[8,256,640]{2,1,0:T(8,128)} %copy-done.1), kind=kLoop, calls=%fused_computation.71 | loop fusion | flops 2359296 | bytes 3145728 | tf_op jit(solution)/shard_map/concatenate | solution.py:70
  145.9 2.5 %fusion.9 = bf16[128,640]{1,0:T(8,128)(2,1)S(1)} fusion(bf16[8,256,640]{2,1,0:T(8,128)(2,1)} %fusion.39, bf16[8,256,128]{1,2,0:T(8,128)(2,1)S(1)} %copy.46, f32[128]{0:T(128)S(1)} %copy-done.8, f32[8,256]{1,0:T(8,128)S(1)} %add_rsqrt_fusion.1, f32[8,256]{1,0:T(8,128)S(1)} %broadcast_multiply_fusion.5), kind=kOutput, calls=%fused_computation.18 | convolution fusion | flops 336936960 | bytes 3326464 | tf_op jit(solution)/shard_map/ijc,ijd->cd/dot_general | solution.py:80
  148.4 0.0 copy-done.6
  148.4 1.1 fusion.17
  149.6 1.9 %fusion.11 = bf16[768,128]{1,0:T(8,128)(2,1)S(1)} fusion(bf16[768,128]{1,0:T(8,128)(2,1)S(1)} %constant_dynamic-update-slice_fusion, bf16[8,256,128]{2,1,0:T(8,128)(2,1)S(1)} %copy-done.4, f32[128]{0:T(128)S(1)} %copy-done.9, f32[8,256]{1,0:T(8,128)S(1)} %add_rsqrt_fusion, f32[8,256]{1,0:T(8,128)S(1)} %broadcast_multiply_fusion.4, ...), kind=kOutput, calls=%fused_computation.21 | convolution fusion | flops 69746688 | bytes 2671104 | tf_op jit(solution)/shard_map/ijh,ijc->hc/dot_general | solution.py:61
  151.5 0.7 pad_maximum_fusion.1
  152.3 6.2 %all-to-all-start.4 = ((bf16[32,26,128]{2,1,0:T(8,128)(2,1)}), bf16[32,26,128]{2,1,0:T(8,128)(2,1)S(1)}, u32[]{:S(2)}, u32[]{:S(2)}) async-start(bf16[32,26,128]{2,1,0:T(8,128)(2,1)} %pad_maximum_fusion.1), calls=%async_computation.4 | async-start | bytes 524288 | tf_op jit(solution)/shard_map/all_to_all | solution.py:22
  158.5 11.9 %all-to-all-done.4 = bf16[32,26,128]{2,1,0:T(8,128)(2,1)S(1)} async-done(((bf16[32,26,128]{2,1,0:T(8,128)(2,1)}), bf16[32,26,128]{2,1,0:T(8,128)(2,1)S(1)}, u32[]{:S(2)}, u32[]{:S(2)}) %all-to-all-start.4) | async-done | bytes 213024 | tf_op jit(solution)/shard_map/all_to_all | solution.py:22
  170.4 0.1 convert_reduce_fusion.1
  170.4 0.7 broadcast_in_dim.5
  171.1 5.0 %all-to-all-start.5 = ((bf16[32,24,128]{2,1,0:T(8,128)(2,1)}), bf16[32,24,128]{2,1,0:T(8,128)(2,1)S(1)}, u32[]{:S(2)}, u32[]{:S(2)}) async-start(bf16[32,24,128]{2,1,0:T(8,128)(2,1)} %broadcast_in_dim.5), calls=%async_computation.5 | async-start | bytes 393216 | tf_op jit(solution)/shard_map/all_to_all | solution.py:22
  176.1 0.3 fusion.16
  176.5 1.0 copy.69
  177.5 0.5 slice_bitcast_fusion.6
  178.0 8.5 %all-to-all-done.5 = bf16[32,24,128]{2,1,0:T(8,128)(2,1)S(1)} async-done(((bf16[32,24,128]{2,1,0:T(8,128)(2,1)}), bf16[32,24,128]{2,1,0:T(8,128)(2,1)S(1)}, u32[]{:S(2)}, u32[]{:S(2)}) %all-to-all-start.5) | async-done | bytes 196640 | tf_op jit(solution)/shard_map/all_to_all | solution.py:22
  186.5 0.6 slice_bitcast_fusion
  187.2 0.0 copy-start.7
  187.2 0.7 copy-done.7
  (30 shorter events, 0.2 us)
Async XLA Ops:
  0.6 1.6 copy-start
  3.8 2.3 %copy-start.1 = (f32[8,256,640]{2,1,0:T(8,128)}, f32[8,256,640]{2,1,0:T(8,128)S(1)}, u32[]{:S(2)}) copy-start(f32[8,256,640]{2,1,0:T(8,128)S(1)} %fusion.54) | copy-start | bytes 15728644
  45.0 23.1 %copy-start.3 = (bf16[8,256,128]{2,1,0:T(8,128)(2,1)S(1)}, bf16[8,256,128]{2,1,0:T(8,128)(2,1)}, u32[]{:S(2)}) copy-start(bf16[8,256,128]{2,1,0:T(8,128)(2,1)} %param.11) | copy-start | bytes 1572868
  45.0 23.1 %copy-start.9 = (f32[128]{0:T(128)S(1)}, f32[128]{0:T(128)}, u32[]{:S(2)}) copy-start(f32[128]{0:T(128)} %param.9) | copy-start | bytes 1540
  45.0 23.1 %copy-start.10 = (bf16[128,128]{1,0:T(8,128)(2,1)S(1)}, bf16[128,128]{1,0:T(8,128)(2,1)}, u32[]{:S(2)}) copy-start(bf16[128,128]{1,0:T(8,128)(2,1)} %param.10) | copy-start | bytes 98308
  96.3 32.0 %all-to-all-start.3 = ((bf16[32,2,4,8,256]{4,3,2,1,0:T(8,128)(2,1)}), bf16[32,2,4,8,256]{4,3,2,1,0:T(8,128)(2,1)S(1)}, u32[]{:S(2)}, u32[]{:S(2)}) async-start(bf16[32,2,4,8,256]{4,3,2,1,0:T(8,128)(2,1)} %copy_bitcast_fusion), calls=%async_computation.3 | async-start | bytes 2097152 | tf_op jit(solution)/shard_map/all_to_all | solution.py:22
  135.2 1.5 copy-start.5
  138.2 5.2 %copy-start.2 = (f32[8,256,128]{2,1,0:T(8,128)S(1)}, f32[8,256,128]{2,1,0:T(8,128)}, u32[]{:S(2)}) copy-start(f32[8,256,128]{2,1,0:T(8,128)} %get-tuple-element.39) | copy-start | bytes 3145732
  138.3 5.2 %copy-start.4 = (bf16[8,256,128]{2,1,0:T(8,128)(2,1)S(1)}, bf16[8,256,128]{2,1,0:T(8,128)(2,1)}, u32[]{:S(2)}) copy-start(bf16[8,256,128]{2,1,0:T(8,128)(2,1)} %param.11) | copy-start | bytes 1572868
  140.7 5.2 %copy-start.8 = (f32[128]{0:T(128)S(1)}, f32[128]{0:T(128)}, u32[]{:S(2)}) copy-start(f32[128]{0:T(128)} %param.7) | copy-start | bytes 1540
  145.9 2.5 %copy-start.6 = (bf16[8,256,640]{2,1,0:T(8,128)(2,1)S(1)}, bf16[8,256,640]{2,1,0:T(8,128)(2,1)}, u32[]{:S(2)}) copy-start(bf16[8,256,640]{2,1,0:T(8,128)(2,1)} %fusion.39) | copy-start | bytes 7864324
  152.3 18.1 %all-to-all-start.4 = ((bf16[32,26,128]{2,1,0:T(8,128)(2,1)}), bf16[32,26,128]{2,1,0:T(8,128)(2,1)S(1)}, u32[]{:S(2)}, u32[]{:S(2)}) async-start(bf16[32,26,128]{2,1,0:T(8,128)(2,1)} %pad_maximum_fusion.1), calls=%async_computation.4 | async-start | bytes 524288 | tf_op jit(solution)/shard_map/all_to_all | solution.py:22
  171.1 15.3 %all-to-all-start.5 = ((bf16[32,24,128]{2,1,0:T(8,128)(2,1)}), bf16[32,24,128]{2,1,0:T(8,128)(2,1)S(1)}, u32[]{:S(2)}, u32[]{:S(2)}) async-start(bf16[32,24,128]{2,1,0:T(8,128)(2,1)} %broadcast_in_dim.5), calls=%async_computation.5 | async-start | bytes 393216 | tf_op jit(solution)/shard_map/all_to_all | solution.py:22
  187.2 0.7 copy-start.7

commit v2 on v1

v2 whole, which is shorter than its diff:
```python
import functools

import jax
import jax.numpy as jnp
from jax import lax
from jax.experimental import pallas as pl
from jax.experimental.pallas import tpu as pltpu
from jax.sharding import PartitionSpec as P

F32, BF16 = jnp.float32, jnp.bfloat16
EPS = 1e-05
LANES = 128


def exchange(values):
    return lax.all_to_all(values, "dap", 0, 0, tiled=True)


def hold(*values):
    return lax.optimization_barrier(values)


def call(kernel, out_shape, operands, scratch=(), flops=0):
    leaves = out_shape if isinstance(out_shape, (tuple, list)) else [out_shape]
    moved = sum(a.size * a.dtype.itemsize for a in list(operands) + list(leaves))
    spec = pl.BlockSpec(memory_space=pltpu.VMEM)
    out_specs = [spec] * len(out_shape) if isinstance(out_shape, (tuple, list)) else spec
    return pl.pallas_call(
        kernel,
        out_shape=out_shape,
        in_specs=[spec] * len(operands),
        out_specs=out_specs,
        scratch_shapes=list(scratch),
        cost_estimate=pl.CostEstimate(flops=flops, bytes_accessed=moved, transcendentals=0),
        compiler_params=pltpu.CompilerParams(vmem_limit_bytes=48 * 1024 * 1024),
    )(*operands)


def norm_rows(values):
    width = values.shape[0]
    shifted = values - jnp.sum(values, axis=0, keepdims=True) * (1.0 / width)
    variance = jnp.sum(shifted * shifted, axis=0, keepdims=True) * (1.0 / width)
    inv_std = lax.rsqrt(variance + EPS)
    return shifted * inv_std, inv_std


def put_row(ref, i, rows, values):
    for h in range(ref.shape[0]):
        spots = pl.ds(i, values.shape[0], stride=rows)
        ref[h, spots, :] = values[:, h * LANES : (h + 1) * LANES]


def take_row(ref, i, rows):
    spots = pl.ds(i, ref.shape[1] // rows, stride=rows)
    return jnp.concatenate([ref[h, spots, :] for h in range(ref.shape[0])], axis=1)


def fill(got_ref, left_ref, right_ref):
    devices, both, _ = got_ref.shape
    half = both // 2
    for n, ref in enumerate((left_ref, right_ref)):
        for h in range(ref.shape[0]):
            block = got_ref[:, n * half : (n + 1) * half, h * LANES : (h + 1) * LANES]
            ref[h] = block.astype(F32).reshape(devices * half, LANES)


def edges_kernel(pair_ref, gain_ref, weight_ref, sent_ref, left_ref, right_ref):
    rows, res, width = pair_ref.shape
    devices = sent_ref.shape[0]
    half = sent_ref.shape[1] // 2
    weight = weight_ref[...].astype(F32).T.astype(BF16)
    gain = gain_ref[...]
    for i in range(rows):
        centred, _ = norm_rows(pair_ref[i].astype(F32).T)
        normed = (centred * gain).astype(BF16)
        out = jnp.dot(weight, normed, preferred_element_type=F32)
        put_row(left_ref, i, rows, jax.nn.sigmoid(out[width : 2 * width]) * out[:width])
        put_row(right_ref, i, rows, jax.nn.sigmoid(out[3 * width :]) * out[2 * width : 3 * width])
    for n, ref in enumerate((left_ref, right_ref)):
        for h in range(res // LANES):
            block = ref[h].reshape(devices, half, LANES).astype(BF16)
            sent_ref[:, n * half : (n + 1) * half, h * LANES : (h + 1) * LANES] = block


def matrices_of(ref, first, share, rows):
    devices, _, res = ref.shape
    block = ref[:, first : first + share * rows, :].astype(F32)
    block = block.reshape(devices, share, rows, res)
    return [block[:, c].reshape(devices * rows, res).astype(BF16) for c in range(share)]


def store_matrices(ref, first, values, rows):
    devices, _, res = ref.shape
    block = jnp.stack([v.reshape(devices, rows, res) for v in values], axis=1)
    ref[:, first : first + len(values) * rows, :] = block.reshape(
        devices, len(values) * rows, res
    ).astype(BF16)


NT = (((1,), (1,)), ((), ()))


def triangle_kernel(share, rows, got_ref, sent_ref):
    half = share * rows
    left = matrices_of(got_ref, 0, share, rows)
    right = matrices_of(got_ref, half, share, rows)
    out = [lax.dot_general(a, b, NT, preferred_element_type=F32) for a, b in zip(left, right)]
    store_matrices(sent_ref, 0, out, rows)


def norm_grad_kernel(rows, got_ref, scaled_ref, sent_ref):
    devices, block, res = got_ref.shape
    share = block // rows
    width = devices * share

    def over_share(values):
        return jnp.sum(values.reshape(share, rows, res), axis=0)

    zero = jnp.zeros((rows, res), F32)

    def add_up(d, carry):
        return carry + over_share(got_ref[d].astype(F32))

    mean = lax.fori_loop(0, devices, add_up, zero, unroll=4) * (1.0 / width)
    mean = jnp.concatenate([mean] * share, axis=0)

    def second(d, carry):
        shifted = got_ref[d].astype(F32) - mean
        return (
            carry[0] + over_share(shifted * shifted),
            carry[1] + over_share(shifted * scaled_ref[d]),
        )

    variance, product = lax.fori_loop(0, devices, second, (zero, zero), unroll=4)
    inv_std = lax.rsqrt(variance * (1.0 / width) + EPS)
    product = product * (1.0 / width) * inv_std * inv_std * inv_std
    inv_std = jnp.concatenate([inv_std] * share, axis=0)
    product = jnp.concatenate([product] * share, axis=0)

    def write(d, carry):
        shifted = got_ref[d].astype(F32) - mean
        sent_ref[d] = (inv_std * scaled_ref[d] - shifted * product).astype(BF16)
        return carry

    lax.fori_loop(0, devices, write, 0, unroll=4)


def edge_grads_kernel(share, rows, got_ref, left_ref, right_ref, sent_ref):
    grads = matrices_of(got_ref, 0, share, rows)
    left_grads, right_grads = [], []
    for c in range(share):
        left_grads.append(jnp.dot(grads[c], right_ref[c], preferred_element_type=F32))
        turned = grads[c].astype(F32).T.astype(BF16)
        right_grads.append(jnp.dot(turned, left_ref[c], preferred_element_type=F32))
    store_matrices(sent_ref, 0, left_grads, rows)
    store_matrices(sent_ref, share * rows, right_grads, rows)


def weight_grads_kernel(got_ref, factor_ref, normed_ref, early_ref, sent_ref, left_ref, right_ref):
    rows, width, _ = normed_ref.shape
    fill(got_ref, left_ref, right_ref)
    total = None
    for i in range(rows):
        left, right = take_row(left_ref, i, rows), take_row(right_ref, i, rows)
        factor = factor_ref[i]
        normed = normed_ref[i]
        parts = []
        for b, grad in enumerate((left, left, right, right)):
            grad = (grad * factor[b * width : (b + 1) * width]).astype(BF16)
            parts.append(lax.dot_general(normed, grad, NT, preferred_element_type=F32))
        total = parts if total is None else [a + b for a, b in zip(total, parts)]
    blocks = jnp.concatenate(total + [early_ref[...]], axis=0)
    sent_ref[...] = blocks.reshape(sent_ref.shape).astype(BF16)


def pair_grad_kernel(
    got_ref, factor_ref, gate_ref, pair_ref, gain_ref, weight_ref, out_ref, left_ref, right_ref
):
    rows, _, width = pair_ref.shape
    fill(got_ref, left_ref, right_ref)
    weight = weight_ref[...]
    gain = gain_ref[...]
    for i in range(rows):
        left, right = take_row(left_ref, i, rows), take_row(right_ref, i, rows)
        factor = factor_ref[i]
        parts = [
            (grad * factor[b * width : (b + 1) * width]).astype(BF16)
            for b, grad in enumerate((left, left, right, right))
        ]
        grads = jnp.concatenate(parts + [gate_ref[i]], axis=0)
        scaled = jnp.dot(weight, grads, preferred_element_type=F32) * gain
        centred, inv_std = norm_rows(pair_ref[i].astype(F32).T)
        first = jnp.sum(scaled, axis=0, keepdims=True) * (1.0 / width)
        second = jnp.sum(scaled * centred, axis=0, keepdims=True) * (1.0 / width)
        grad_pair = inv_std * (scaled - first - centred * second)
        out_ref[i] = grad_pair.T.astype(BF16)


def finish_kernel(full_ref, weight_ref, w_out_ref, gain_in_ref, gain_out_ref, *outs):
    grad_weight_ref, grad_out_ref, grad_gain_in_ref, grad_gain_out_ref = outs
    width = w_out_ref.shape[0]
    full = full_ref[...].astype(F32).reshape(6 * width, width)
    weight = weight_ref[...].astype(F32)
    total = jnp.zeros((width, width), F32)
    for b in range(5):
        block = full[b * width : (b + 1) * width]
        grad_weight_ref[:, b * width : (b + 1) * width] = block
        total = total + block * weight[:, b * width : (b + 1) * width]
    block = full[5 * width :]
    grad_out_ref[...] = block
    total_out = block * w_out_ref[...].astype(F32)
    grad_gain_in_ref[...] = jnp.sum(total.T, axis=0, keepdims=True) / gain_in_ref[...]
    grad_gain_out_ref[...] = jnp.sum(total_out.T, axis=0, keepdims=True) / gain_out_ref[...]


def local(devices, pair, gain_in, w_proj, gain_out, w_out, cotangent):
    width = gain_out.shape[0]
    rows, res, _ = pair.shape
    share = width // devices
    half = share * rows
    shape = jax.ShapeDtypeStruct
    scratch = [pltpu.VMEM((res // LANES, width * rows, LANES), F32)] * 2

    def mean_c(values):
        return jnp.mean(values, axis=1, keepdims=True)

    def channel_norm(values):
        shifted = values - mean_c(values)
        inv_std = lax.rsqrt(mean_c(shifted * shifted) + EPS)
        return shifted * inv_std, inv_std

    gain_in_col, gain_out_col = gain_in[:, None], gain_out[:, None]
    sent = call(
        edges_kernel,
        shape((devices, 2 * half, res), BF16),
        (pair, gain_in_col, w_proj[:, : 4 * width]),
        scratch,
    )
    sent, pair, cotangent = hold(sent, pair, cotangent)
    got = exchange(sent)

    centred, _ = channel_norm(pair.transpose(0, 2, 1).astype(F32))
    normed = (centred * gain_in_col[None]).astype(BF16)
    projected = jnp.einsum("cd,ick->idk", w_proj, normed, preferred_element_type=F32)
    left_val, left_gate, right_val, right_gate, out_gate = [
        projected[:, b * width : (b + 1) * width] for b in range(5)
    ]
    left_sig, right_sig = jax.nn.sigmoid(left_gate), jax.nn.sigmoid(right_gate)
    factor = jnp.concatenate(
        [
            left_sig,
            left_val * left_sig * (1.0 - left_sig),
            right_sig,
            right_val * right_sig * (1.0 - right_sig),
        ],
        axis=1,
    )
    out_gate = jax.nn.sigmoid(out_gate)
    cot = cotangent.transpose(0, 2, 1).astype(F32)
    grad_proj_out = (cot * out_gate).astype(BF16)
    scaled = jnp.einsum("hc,ick->ihk", w_out, grad_proj_out, preferred_element_type=F32)
    scaled = scaled * gain_out_col[None]
    scaled = scaled - mean_c(scaled)
    scaled = scaled.transpose(1, 0, 2).reshape(devices, half, res)

    got, normed, factor, out_gate, cot, grad_proj_out, scaled = hold(
        got, normed, factor, out_gate, cot, grad_proj_out, scaled
    )
    sent = call(
        functools.partial(triangle_kernel, share, rows), shape((devices, half, res), BF16), (got,)
    )
    sent, got = hold(sent, got)
    edges = got.reshape(devices, 2, share, rows, res).transpose(1, 2, 0, 3, 4)
    edges = edges.reshape(2, share, devices * rows, res)
    got = exchange(sent)
    got, edges = hold(got, edges)
    sent = call(
        functools.partial(norm_grad_kernel, rows),
        shape((devices, half, res), BF16),
        (got, scaled),
    )
    sent, triangle = hold(sent, got)
    got = exchange(sent)

    triangle = triangle.reshape(width, rows, res).transpose(1, 0, 2).astype(F32)
    tri_centred, _ = channel_norm(triangle)
    out_normed = (tri_centred * gain_out_col[None]).astype(BF16)
    out_proj = jnp.einsum("hc,ihk->ick", w_out, out_normed, preferred_element_type=F32)
    update = (out_gate * out_proj).astype(BF16).transpose(0, 2, 1)
    grad_gate = (cot * out_proj * out_gate * (1.0 - out_gate)).astype(BF16)
    grad_w_gate = jnp.einsum("ick,idk->cd", normed, grad_gate, preferred_element_type=F32)
    grad_w_out = jnp.einsum("ihk,ick->hc", out_normed, grad_proj_out, preferred_element_type=F32)
    early = jnp.concatenate([grad_w_gate, grad_w_out], axis=0)
    got, early, grad_gate, update = hold(got, early, grad_gate, update)

    sent = call(
        functools.partial(edge_grads_kernel, share, rows),
        shape((devices, 2 * half, res), BF16),
        (got, edges[0], edges[1]),
    )
    got = exchange(sent)
    sent = call(
        weight_grads_kernel,
        shape((devices, 6 * width // devices, width), BF16),
        (got, factor, normed, early),
        scratch,
    )
    sent, edge_grads, factor = hold(sent, got, factor)
    got = exchange(sent)
    grad_pair = call(
        pair_grad_kernel,
        shape((rows, res, width), BF16),
        (edge_grads, factor, grad_gate, pair, gain_in_col, w_proj),
        scratch,
        flops=2 * rows * res * width * 5 * width,
    )
    mine = jnp.sum(got.astype(F32), axis=0).astype(BF16)
    full = exchange(jnp.broadcast_to(mine[None], (devices,) + mine.shape))
    grad_w_proj, grad_w_out, grad_gain_in, grad_gain_out = call(
        finish_kernel,
        (
            shape((width, 5 * width), F32),
            shape((width, width), F32),
            shape((1, width), F32),
            shape((1, width), F32),
        ),
        (full, w_proj, w_out, gain_in[None], gain_out[None]),
    )
    return (update, grad_pair, grad_gain_in[0], grad_w_proj, grad_gain_out[0], grad_w_out)


def solution(mesh):
    devices = mesh.shape["dap"]

    def program(*args):
        return local(devices, *args)

    in_specs = (P(("dp", "dap"), None, None), P(), P(), P(), P(), P(("dp", "dap"), None, None))
    out_specs = (
        P(("dp", "dap"), None, None),
        P(("dp", "dap"), None, None),
        P("dp"),
        P("dp", None),
        P("dp"),
        P("dp", None),
    )
    return jax.shard_map(program, mesh=mesh, in_specs=in_specs, out_specs=out_specs, check_vma=False)
```

time: 189 us -> 159 us (0.84)
  blocking collectives: 81.4 us -> 47.6 us
  Pallas kernels: 0 us -> 11.6 us
  starting transfers between devices: 16.9 us -> 28.1 us
  matrix products: 13.3 us -> 3.32 us
  other arithmetic: 16.3 us -> 6.53 us
  waiting for transfers between devices: 43.8 us -> 50.4 us
  local copies, waits for them, and re-layouts: 15.3 us -> 9.8 us
    all_to_all x3 -> x2, blocking collectives: 81.4 us -> 47.6 us  [exchange(): return lax.all_to_all(values, 'dap', 0, 0, tiled=True)]
    pallas_call x0 -> x7, Pallas kernels: none -> 11.6 us  [call(): pl.pallas_call(kernel, out_shape=out_shape, in_specs=[spec] * len(operand...]
    all_to_all x3 -> x4, starting transfers between devices: 16.9 us -> 28.1 us  [exchange(): return lax.all_to_all(values, 'dap', 0, 0, tiled=True)]
    dot_general x9 -> x5, matrix products: 13.3 us -> 3.32 us  [the longest x1 1.38 us: local(): jnp.einsum('hc,ihk->ick', w_out, out_normed, preferred_element_type=F32)]
    unnamed x4 -> x0, other arithmetic: 8.63 us -> none
    all_to_all x3 -> x4, waiting for transfers between devices: 43.8 us -> 50.4 us  [exchange(): return lax.all_to_all(values, 'dap', 0, 0, tiled=True)]
    squeeze x4 -> x1, local copies, waits for them, and re-layouts: 4.31 us -> 0.07 us  [local(): edges[1]]
    unnamed x33 -> x27, local copies, waits for them, and re-layouts: 6.38 us -> 4.1 us
  transfers between devices with their start and end apart: 3 -> 4, of which waited for: 3 -> 4; matrix products, arithmetic and copies ran while one was open for 3% -> 9% of each run, Pallas kernels for 0% -> 3%
where the time goes in v2:
time: 159 us; the launch traced here: 158 us
  waiting for transfers between devices  50.4 us (32%)
  blocking collectives  47.6 us (30%)
  starting transfers between devices  28.1 us (18%)
  Pallas kernels  11.6 us (7%)
  local copies, waits for them, and re-layouts  9.8 us (6%)
  other arithmetic  6.53 us (4%)
  matrix products  3.32 us (2%)
    all_to_all x4, waiting for transfers between devices, exchange(): return lax.all_to_all(values, 'dap', 0, 0, tiled=True)  50.4 us
    all_to_all x2, blocking collectives, exchange(): return lax.all_to_all(values, 'dap', 0, 0, tiled=True)  47.6 us
    all_to_all x4, starting transfers between devices, exchange(): return lax.all_to_all(values, 'dap', 0, 0, tiled=True)  28.1 us
    pallas_call x7, Pallas kernels, call(): pl.pallas_call(kernel, out_shape=out_shape, in_specs=[spec] * len(operand...  11.6 us
    unnamed x27, local copies, waits for them, and re-layouts  4.1 us
  transfers between devices with their start and end apart: 4, of which 4 were waited for; matrix products, arithmetic and copies ran while one was open for 9% of the time, Pallas kernels for 3%

profile of v2, /device:TPU:1, one launch (start us, length us, event | category | flops | bytes accessed | tf_op | source)
XLA Modules:
  0.0 158.3 jit_solution(13641855766818775541)
XLA Ops:
  0.6 0.0 copy-start.7
  0.6 0.8 copy.12.gain_ref
  1.5 0.0 copy-start.4
  1.5 1.0 slice.24.weight_ref
  2.5 0.0 copy-start.1
  2.5 1.0 copy-done.1
  3.5 0.0 copy-start.2
  3.5 2.2 %shard_map.109 = bf16[32,64,256]{2,1,0:T(8,128)(2,1)} custom-call(bf16[8,256,128]{2,1,0:T(8,128)(2,1)S(1)} %copy-done.1, f32[128,1]{1,0:T(8,128)S(1)} %copy.12.gain_ref, bf16[128,512]{1,0:T(8,128)(2,1)S(1)} %slice.24.weight_ref), custom_call_target="tpu_custom_call" | custom-call | bytes 1704448 | tf_op jit(solution)/shard_map/pallas_call | solution.py:28
  5.7 11.1 %all-to-all-start = ((bf16[32,64,256]{2,1,0:T(8,128)(2,1)}), bf16[32,64,256]{2,1,0:T(8,128)(2,1)S(1)}, u32[]{:S(2)}, u32[]{:S(2)}) async-start(bf16[32,64,256]{2,1,0:T(8,128)(2,1)} %shard_map.109), calls=%async_computation | async-start | bytes 2097152 | tf_op jit(solution)/shard_map/all_to_all | solution.py:16
  16.8 0.0 copy-done.2
  16.9 0.2 copy.13
  17.1 0.1 bitcast_reduce_fusion.1
  17.2 0.2 fusion.13
  17.3 0.0 copy-done.7
  17.4 0.2 fusion.15.normed_ref
  17.5 0.0 copy-done.12
  17.5 0.2 copy.16
  17.8 0.0 copy-done.4
  17.8 0.9 convolution_bitcast_fusion
  18.7 0.0 copy-start.5
  18.7 0.0 copy-start.6
  18.7 2.0 %multiply_convert_fusion.3 = (bf16[8,128,256]{2,1,0:T(8,128)(2,1)S(1)}, f32[8,128,256]{2,1,0:T(8,128)}, f32[8,128,256]{2,1,0:T(8,128)S(1)}, f32[8,128,256]{2,1,0...) fusion(bf16[8,256,128]{1,2,0:T(8,128)(2,1)S(1)} %copy.16, ...), kind=kLoop, calls=%fused_computation.38 | loop fusion | flops 4718592 | bytes 11534336 | tf_op jit(solution)/shard_map/convert_element_type | solution.py:260
  20.7 0.0 copy-done.5
  20.7 0.0 copy-done.6
  20.7 0.3 fusion.20
  21.0 0.1 subtract_bitcast_fusion
  21.1 1.6 %copy.17 = f32[128,8,256]{2,1,0:T(8,128)} copy(f32[128,8,256]{2,0,1:T(8,128)S(1)} %subtract_bitcast_fusion) | data formatting | bytes 2097152 | tf_op jit(solution)/shard_map/sub | solution.py:263
  22.7 2.2 %pad_maximum_fusion.factor_ref = f32[8,512,256]{2,1,0:T(8,128)} fusion(f32[8,128,256]{2,1,0:T(8,128)S(1)} %get-tuple-element.68, f32[8,128,256]{2,1,0:T(8,128)S(1)} %get-tuple-element.69, f32[8,128,256]{2,1,0:T(8,128)S(1)} %get-tuple-element.70, f32[8,128,256]{2,1,0:T(8,128)S(1)} %get-tuple-element.71), kind=kLoop, calls=%fused_computation | loop fusion | flops 3145728 | bytes 8388608 | tf_op jit(solution)/shard_map/concatenate | solution.py:249
  24.9 1.1 convert_bitcast_fusion
  26.0 17.3 %all-to-all-done.got_ref = bf16[32,64,256]{2,1,0:T(8,128)(2,1)S(1)} async-done(((bf16[32,64,256]{2,1,0:T(8,128)(2,1)}), bf16[32,64,256]{2,1,0:T(8,128)(2,1)S(1)}, u32[]{:S(2)}, u32[]{:S(2)}) %all-to-all-start) | async-done | bytes 1048608 | tf_op jit(solution)/shard_map/all_to_all | solution.py:16
  43.3 1.1 shard_map.110
  44.4 6.0 %all-to-all-start.1 = ((bf16[32,32,256]{2,1,0:T(8,128)(2,1)}), bf16[32,32,256]{2,1,0:T(8,128)(2,1)S(1)}, u32[]{:S(2)}, u32[]{:S(2)}) async-start(bf16[32,32,256]{2,1,0:T(8,128)(2,1)} %shard_map.110), calls=%async_computation.1 | async-start | bytes 1048576 | tf_op jit(solution)/shard_map/all_to_all | solution.py:16
  50.4 1.1 copy.36
  51.5 15.5 %all-to-all-done.1.got_ref = bf16[32,32,256]{2,1,0:T(8,128)(2,1)S(1)} async-done(((bf16[32,32,256]{2,1,0:T(8,128)(2,1)}), bf16[32,32,256]{2,1,0:T(8,128)(2,1)S(1)}, u32[]{:S(2)}, u32[]{:S(2)}) %all-to-all-start.1) | async-done | bytes 524320 | tf_op jit(solution)/shard_map/all_to_all | solution.py:16
  67.0 1.2 copy-done.3
  68.2 1.4 shard_map.111
  69.6 5.7 %all-to-all-start.2 = ((bf16[32,32,256]{2,1,0:T(8,128)(2,1)}), bf16[32,32,256]{2,1,0:T(8,128)(2,1)S(1)}, u32[]{:S(2)}, u32[]{:S(2)}) async-start(bf16[32,32,256]{2,1,0:T(8,128)(2,1)} %shard_map.111), calls=%async_computation.2 | async-start | bytes 1048576 | tf_op jit(solution)/shard_map/all_to_all | solution.py:16
  75.3 0.0 copy-start.8
  75.3 0.0 copy-start.10
  75.3 0.1 convert.5
  75.4 0.3 bitcast_reduce_fusion
  75.7 0.0 copy-start.9
  75.7 0.3 multiply_reduce_fusion
  76.0 0.5 copy-done.8
  76.5 0.3 copy-done.10
  76.8 1.4 fusion.16
  78.2 0.3 convolution_bitcast_fusion.3
  78.5 0.5 convolution_bitcast_fusion.2
  79.0 0.0 copy-done.9
  79.0 0.1 slice_bitcast_fusion
  79.1 12.9 %all-to-all-done.2.got_ref = bf16[32,32,256]{2,1,0:T(8,128)(2,1)S(1)} async-done(((bf16[32,32,256]{2,1,0:T(8,128)(2,1)}), bf16[32,32,256]{2,1,0:T(8,128)(2,1)S(1)}, u32[]{:S(2)}, u32[]{:S(2)}) %all-to-all-start.2) | async-done | bytes 524320 | tf_op jit(solution)/shard_map/all_to_all | solution.py:16
  92.0 0.5 shard_map.112
  92.5 0.0 copy-start.11
  92.5 31.5 %all_to_all.30.got_ref = bf16[32,64,256]{2,1,0:T(8,128)(2,1)S(1)} all-to-all(bf16[32,64,256]{2,1,0:T(8,128)(2,1)S(1)} %shard_map.112), channel_id=1, replica_groups=mesh['dp'=8,'dap'=32] {'dap'}, dimensions={0} | all-to-all | bytes 2097152 | tf_op jit(solution)/shard_map/all_to_all | solution.py:16
  124.0 0.0 copy-done
  124.0 1.0 shard_map.113
  125.0 16.1 %all_to_all.31 = bf16[32,24,128]{2,1,0:T(8,128)(2,1)S(1)} all-to-all(bf16[32,24,128]{2,1,0:T(8,128)(2,1)S(1)} %shard_map.113), channel_id=1, replica_groups=mesh['dp'=8,'dap'=32] {'dap'}, dimensions={0} | all-to-all | bytes 393216 | tf_op jit(solution)/shard_map/all_to_all | solution.py:16
  141.1 0.7 broadcast_in_dim.9
  141.8 5.4 %all-to-all-start.5 = ((bf16[32,24,128]{2,1,0:T(8,128)(2,1)}), bf16[32,24,128]{2,1,0:T(8,128)(2,1)S(1)}, u32[]{:S(2)}, u32[]{:S(2)}) async-start(bf16[32,24,128]{2,1,0:T(8,128)(2,1)} %broadcast_in_dim.9), calls=%async_computation.5 | async-start | bytes 393216 | tf_op jit(solution)/shard_map/all_to_all | solution.py:16
  147.2 0.0 copy-done.11
  147.2 1.0 copy.23
  148.2 4.6 %shard_map.114 = bf16[8,256,128]{2,1,0:T(8,128)(2,1)} custom-call(bf16[32,64,256]{2,1,0:T(8,128)(2,1)S(1)} %all_to_all.30.got_ref, f32[8,512,256]{2,1,0:T(8,128)} %pad_maximum_fusion.factor_ref, bf16[8,128,256]{2,1,0:T(8,128)(2,1)S(1)} %get-tuple-element.54.gate_ref, bf16[8,256,128]{2,1,0:T(8,128)(2,1)S(1)} %copy-done.2, f32[128,1]{1,0:T(8,128)S(1)} %copy.12.gain_ref, ...), custom_call_target="tpu_custom_call" | custom-call | flops 335544320 | bytes 6980096 | tf_op jit(solution)/shard_map/pallas_call | solution.py:28
  152.8 4.7 %all-to-all-done.5.full_ref = bf16[32,24,128]{2,1,0:T(8,128)(2,1)S(1)} async-done(((bf16[32,24,128]{2,1,0:T(8,128)(2,1)}), bf16[32,24,128]{2,1,0:T(8,128)(2,1)S(1)}, u32[]{:S(2)}, u32[]{:S(2)}) %all-to-all-start.5) | async-done | bytes 196640 | tf_op jit(solution)/shard_map/all_to_all | solution.py:16
  157.5 0.8 shard_map.115
  (10 shorter events, 0.1 us)
Async XLA Ops:
  0.6 16.7 %copy-start.7 = (f32[128]{0:T(128)S(1)}, f32[128]{0:T(128)}, u32[]{:S(2)}) copy-start(f32[128]{0:T(128)} %param.7) | copy-start | bytes 1540
  1.5 16.3 %copy-start.4 = (bf16[128,640]{1,0:T(8,128)(2,1)S(1)}, bf16[128,640]{1,0:T(8,128)(2,1)}, u32[]{:S(2)}) copy-start(bf16[128,640]{1,0:T(8,128)(2,1)} %weight_ref.3) | copy-start | bytes 491524
  2.5 1.0 copy-start.1
  3.5 13.3 %copy-start.2 = (bf16[8,256,128]{2,1,0:T(8,128)(2,1)S(1)}, bf16[8,256,128]{2,1,0:T(8,128)(2,1)}, u32[]{:S(2)}) copy-start(bf16[8,256,128]{2,1,0:T(8,128)(2,1)} %pair_ref.2) | copy-start | bytes 1572868
  3.5 14.0 %copy-start.12 = (bf16[8,256,128]{2,1,0:T(8,128)(2,1)S(1)}, bf16[8,256,128]{2,1,0:T(8,128)(2,1)}, u32[]{:S(2)}) copy-start(bf16[8,256,128]{2,1,0:T(8,128)(2,1)} %param.11) | copy-start | bytes 1572868
  5.7 37.6 %all-to-all-start = ((bf16[32,64,256]{2,1,0:T(8,128)(2,1)}), bf16[32,64,256]{2,1,0:T(8,128)(2,1)S(1)}, u32[]{:S(2)}, u32[]{:S(2)}) async-start(bf16[32,64,256]{2,1,0:T(8,128)(2,1)} %shard_map.109), calls=%async_computation | async-start | bytes 2097152 | tf_op jit(solution)/shard_map/all_to_all | solution.py:16
  18.7 2.0 %copy-start.5 = (bf16[128,128]{1,0:T(8,128)(2,1)S(1)}, bf16[128,128]{1,0:T(8,128)(2,1)}, u32[]{:S(2)}) copy-start(bf16[128,128]{1,0:T(8,128)(2,1)} %w_out_ref.1) | copy-start | bytes 98308
  18.7 2.0 %copy-start.6 = (f32[128]{0:T(128)S(1)}, f32[128]{0:T(128)}, u32[]{:S(2)}) copy-start(f32[128]{0:T(128)} %param.9) | copy-start | bytes 1540
  44.4 22.6 %all-to-all-start.1 = ((bf16[32,32,256]{2,1,0:T(8,128)(2,1)}), bf16[32,32,256]{2,1,0:T(8,128)(2,1)S(1)}, u32[]{:S(2)}, u32[]{:S(2)}) async-start(bf16[32,32,256]{2,1,0:T(8,128)(2,1)} %shard_map.110), calls=%async_computation.1 | async-start | bytes 1048576 | tf_op jit(solution)/shard_map/all_to_all | solution.py:16
  67.0 1.2 copy-start.3
  69.6 22.4 %all-to-all-start.2 = ((bf16[32,32,256]{2,1,0:T(8,128)(2,1)}), bf16[32,32,256]{2,1,0:T(8,128)(2,1)S(1)}, u32[]{:S(2)}, u32[]{:S(2)}) async-start(bf16[32,32,256]{2,1,0:T(8,128)(2,1)} %shard_map.111), calls=%async_computation.2 | async-start | bytes 1048576 | tf_op jit(solution)/shard_map/all_to_all | solution.py:16
  75.3 1.2 copy-start.8
  75.3 1.5 copy-start.10
  75.7 3.3 %copy-start.9 = (bf16[32,2,4,8,256]{4,3,0,2,1:T(8,128)(2,1)S(1)}, bf16[32,2,4,8,256]{4,3,0,2,1:T(8,128)(2,1)}, u32[]{:S(2)}) copy-start(bf16[32,2,4,8,256]{4,3,0,2,1:T(8,128)(2,1)} %copy.36) | copy-start | bytes 3145732
  92.0 32.0 %copy-start = (f32[8,512,256]{2,1,0:T(8,128)S(1)}, f32[8,512,256]{2,1,0:T(8,128)}, u32[]{:S(2)}) copy-start(f32[8,512,256]{2,1,0:T(8,128)} %pad_maximum_fusion.factor_ref) | copy-start | bytes 12582916
  92.5 54.7 %copy-start.11 = (bf16[8,256,128]{1,2,0:T(8,128)(2,1)S(1)}, bf16[8,256,128]{1,2,0:T(8,128)(2,1)}, u32[]{:S(2)}) copy-start(bf16[8,256,128]{1,2,0:T(8,128)(2,1)} %get-tuple-element.60) | copy-start | bytes 1572868
  141.8 15.7 %all-to-all-start.5 = ((bf16[32,24,128]{2,1,0:T(8,128)(2,1)}), bf16[32,24,128]{2,1,0:T(8,128)(2,1)S(1)}, u32[]{:S(2)}, u32[]{:S(2)}) async-start(bf16[32,24,128]{2,1,0:T(8,128)(2,1)} %broadcast_in_dim.9), calls=%async_computation.5 | async-start | bytes 393216 | tf_op jit(solution)/shard_map/all_to_all | solution.py:16

commit v3 on v2

v3 whole, which is shorter than its diff:
```python
import functools

import jax
import jax.numpy as jnp
from jax import lax
from jax.experimental import pallas as pl
from jax.experimental.pallas import tpu as pltpu
from jax.sharding import PartitionSpec as P

F32, BF16 = jnp.float32, jnp.bfloat16
EPS = 1e-05
LANES = 128
NT = (((1,), (1,)), ((), ()))


def exchange(values):
    return lax.all_to_all(values, "dap", 0, 0, tiled=True)


def hold(*values):
    return lax.optimization_barrier(values)


def call(kernel, out_shape, operands, scratch=(), flops=0, outside=0, limit=16):
    leaves = out_shape if isinstance(out_shape, (tuple, list)) else [out_shape]
    moved = sum(a.size * a.dtype.itemsize for a in list(operands) + list(leaves))
    spec = pl.BlockSpec(memory_space=pltpu.VMEM)
    out_specs = [spec] * len(out_shape) if isinstance(out_shape, (tuple, list)) else spec
    return pl.pallas_call(
        kernel,
        out_shape=out_shape,
        in_specs=[pl.BlockSpec(memory_space=pltpu.HBM)] * outside + [spec] * (len(operands) - outside),
        out_specs=out_specs,
        scratch_shapes=list(scratch),
        cost_estimate=pl.CostEstimate(flops=flops, bytes_accessed=moved, transcendentals=0),
        compiler_params=pltpu.CompilerParams(vmem_limit_bytes=limit * 1024 * 1024),
    )(*operands)


def norm_rows(values):
    width = values.shape[0]
    shifted = values - jnp.sum(values, axis=0, keepdims=True) * (1.0 / width)
    variance = jnp.sum(shifted * shifted, axis=0, keepdims=True) * (1.0 / width)
    inv_std = lax.rsqrt(variance + EPS)
    return shifted * inv_std, inv_std


def put_row(ref, i, rows, values):
    for h in range(ref.shape[0]):
        spots = pl.ds(i, values.shape[0], stride=rows)
        ref[h, spots, :] = values[:, h * LANES : (h + 1) * LANES]


def take_row(ref, i, rows):
    spots = pl.ds(i, ref.shape[1] // rows, stride=rows)
    return jnp.concatenate([ref[h, spots, :] for h in range(ref.shape[0])], axis=1)


def fill(got_ref, left_ref, right_ref):
    devices, both, _ = got_ref.shape
    half = both // 2
    for n, ref in enumerate((left_ref, right_ref)):
        for h in range(ref.shape[0]):
            block = got_ref[:, n * half : (n + 1) * half, h * LANES : (h + 1) * LANES]
            ref[h] = block.astype(F32).reshape(devices * half, LANES)


def edges_kernel(
    pair_hbm, gain_hbm, weight_hbm, sent_ref, left_ref, right_ref, pair_ref, gain_ref, weight_ref, sems
):
    rows, res, width = pair_ref.shape
    devices = sent_ref.shape[0]
    half = sent_ref.shape[1] // 2
    pairs = ((weight_hbm, weight_ref), (gain_hbm, gain_ref), (pair_hbm, pair_ref))
    copies = [
        pltpu.make_async_copy(source, target, sems.at[n])
        for n, (source, target) in enumerate(pairs)
    ]
    for copy in copies:
        copy.start()
    copies[0].wait()
    weight = weight_ref[:, : 4 * width].astype(F32).T.astype(BF16)
    copies[1].wait()
    gain = gain_ref[...].T
    copies[2].wait()
    for i in range(rows):
        centred, _ = norm_rows(pair_ref[i].astype(F32).T)
        normed = (centred * gain).astype(BF16)
        out = jnp.dot(weight, normed, preferred_element_type=F32)
        put_row(left_ref, i, rows, jax.nn.sigmoid(out[width : 2 * width]) * out[:width])
        put_row(right_ref, i, rows, jax.nn.sigmoid(out[3 * width :]) * out[2 * width : 3 * width])
    for n, ref in enumerate((left_ref, right_ref)):
        for h in range(res // LANES):
            block = ref[h].reshape(devices, half, LANES).astype(BF16)
            sent_ref[:, n * half : (n + 1) * half, h * LANES : (h + 1) * LANES] = block


def prepare_kernel(
    pair_ref,
    cot_ref,
    gain_in_ref,
    gain_out_ref,
    weight_ref,
    w_out_ref,
    normed_ref,
    factor_ref,
    grad_out_ref,
    scaled_ref,
):
    rows, res, width = pair_ref.shape
    weight = weight_ref[...].astype(F32).T.astype(BF16)
    w_out = w_out_ref[...]
    gain_in, gain_out = gain_in_ref[...].T, gain_out_ref[...].T
    for i in range(rows):
        centred, _ = norm_rows(pair_ref[i].astype(F32).T)
        normed = (centred * gain_in).astype(BF16)
        normed_ref[i] = normed
        out = jnp.dot(weight, normed, preferred_element_type=F32)
        for side in range(2):
            first = 2 * side * width
            sig = jax.nn.sigmoid(out[first + width : first + 2 * width])
            factor_ref[i, first : first + width, :] = sig
            factor_ref[i, first + width : first + 2 * width, :] = (
                out[first : first + width] * sig * (1.0 - sig)
            )
        gate = jax.nn.sigmoid(out[4 * width :])
        factor_ref[i, 4 * width :, :] = gate
        grad_out = (cot_ref[i].astype(F32).T * gate).astype(BF16)
        grad_out_ref[i] = grad_out
        scaled = jnp.dot(w_out, grad_out, preferred_element_type=F32) * gain_out
        scaled = scaled - jnp.sum(scaled, axis=0, keepdims=True) * (1.0 / width)
        put_row(scaled_ref, i, rows, scaled)


def matrices_of(ref, first, share, rows):
    devices, _, res = ref.shape
    block = ref[:, first : first + share * rows, :].astype(F32)
    block = block.reshape(devices, share, rows, res)
    return [block[:, c].reshape(devices * rows, res).astype(BF16) for c in range(share)]


def store_matrices(ref, first, values, rows):
    devices, _, res = ref.shape
    block = jnp.stack([v.reshape(devices, rows, res) for v in values], axis=1)
    ref[:, first : first + len(values) * rows, :] = block.reshape(
        devices, len(values) * rows, res
    ).astype(BF16)


def triangle_kernel(share, rows, got_ref, sent_ref, left_ref, right_ref):
    half = share * rows
    left = matrices_of(got_ref, 0, share, rows)
    right = matrices_of(got_ref, half, share, rows)
    for c in range(share):
        left_ref[c] = left[c]
        right_ref[c] = right[c]
    out = [lax.dot_general(a, b, NT, preferred_element_type=F32) for a, b in zip(left, right)]
    store_matrices(sent_ref, 0, out, rows)


def norm_grad_kernel(rows, got_ref, scaled_ref, sent_ref):
    devices, block, res = got_ref.shape
    share = block // rows
    width = devices * share

    def over_share(values):
        return jnp.sum(values.reshape(share, rows, res), axis=0)

    zero = jnp.zeros((rows, res), F32)

    def scaled_of(d):
        spots = pl.ds(pl.multiple_of(d * block, block), block)
        return jnp.concatenate([scaled_ref[h, spots, :] for h in range(res // LANES)], axis=1)

    def add_up(d, carry):
        return carry + over_share(got_ref[d].astype(F32))

    mean = lax.fori_loop(0, devices, add_up, zero, unroll=4) * (1.0 / width)
    mean = jnp.concatenate([mean] * share, axis=0)

    def second(d, carry):
        shifted = got_ref[d].astype(F32) - mean
        return (
            carry[0] + over_share(shifted * shifted),
            carry[1] + over_share(shifted * scaled_of(d)),
        )

    variance, product = lax.fori_loop(0, devices, second, (zero, zero), unroll=4)
    inv_std = lax.rsqrt(variance * (1.0 / width) + EPS)
    product = product * (1.0 / width) * inv_std * inv_std * inv_std
    inv_std = jnp.concatenate([inv_std] * share, axis=0)
    product = jnp.concatenate([product] * share, axis=0)

    def write(d, carry):
        shifted = got_ref[d].astype(F32) - mean
        sent_ref[d] = (inv_std * scaled_of(d) - shifted * product).astype(BF16)
        return carry

    lax.fori_loop(0, devices, write, 0, unroll=4)


def edge_grads_kernel(share, rows, got_ref, left_ref, right_ref, sent_ref):
    grads = matrices_of(got_ref, 0, share, rows)
    left_grads, right_grads = [], []
    for c in range(share):
        left_grads.append(jnp.dot(grads[c], right_ref[c], preferred_element_type=F32))
        turned = grads[c].astype(F32).T.astype(BF16)
        right_grads.append(jnp.dot(turned, left_ref[c], preferred_element_type=F32))
    store_matrices(sent_ref, 0, left_grads, rows)
    store_matrices(sent_ref, share * rows, right_grads, rows)


def turn(triangle_ref, turned_ref):
    devices, half, _ = triangle_ref.shape
    for h in range(turned_ref.shape[0]):
        block = triangle_ref[:, :, h * LANES : (h + 1) * LANES]
        turned_ref[h] = block.astype(F32).reshape(devices * half, LANES)


def gate_grads(i, rows, factor_ref, cot_ref, gain_out, w_out, turned_ref):
    width = w_out.shape[0]
    centred, _ = norm_rows(take_row(turned_ref, i, rows))
    out_normed = (centred * gain_out).astype(BF16)
    gate = factor_ref[i, 4 * width :, :]
    update = gate * jnp.dot(w_out, out_normed, preferred_element_type=F32)
    grad_gate = (cot_ref[i].astype(F32).T * update * (1.0 - gate)).astype(BF16)
    return out_normed, update, grad_gate


def edge_parts(i, rows, factor_ref, left_ref, right_ref):
    left, right = take_row(left_ref, i, rows), take_row(right_ref, i, rows)
    width = left.shape[0]
    return [
        (grad * factor_ref[i, b * width : (b + 1) * width, :]).astype(BF16)
        for b, grad in enumerate((left, left, right, right))
    ]


def weight_grads_kernel(
    got_ref,
    factor_ref,
    normed_ref,
    triangle_ref,
    cot_ref,
    grad_out_ref,
    gain_out_ref,
    w_out_ref,
    sent_ref,
    left_ref,
    right_ref,
    turned_ref,
):
    rows = normed_ref.shape[0]
    fill(got_ref, left_ref, right_ref)
    turn(triangle_ref, turned_ref)
    w_out = w_out_ref[...].astype(F32).T.astype(BF16)
    gain_out = gain_out_ref[...].T
    total = None
    for i in range(rows):
        out_normed, _, grad_gate = gate_grads(
            i, rows, factor_ref, cot_ref, gain_out, w_out, turned_ref
        )
        grads = edge_parts(i, rows, factor_ref, left_ref, right_ref) + [grad_gate]
        pairs = [(normed_ref[i], grad) for grad in grads] + [(out_normed, grad_out_ref[i])]
        parts = [lax.dot_general(x, y, NT, preferred_element_type=F32) for x, y in pairs]
        total = parts if total is None else [x + y for x, y in zip(total, parts)]
    sent_ref[...] = jnp.concatenate(total, axis=0).reshape(sent_ref.shape).astype(BF16)


def pair_grad_kernel(
    got_ref,
    factor_ref,
    pair_ref,
    triangle_ref,
    cot_ref,
    gain_in_ref,
    gain_out_ref,
    weight_ref,
    w_out_ref,
    out_ref,
    update_ref,
    left_ref,
    right_ref,
    turned_ref,
):
    rows, _, width = pair_ref.shape
    fill(got_ref, left_ref, right_ref)
    turn(triangle_ref, turned_ref)
    weight = weight_ref[...]
    w_out = w_out_ref[...].astype(F32).T.astype(BF16)
    gain_in, gain_out = gain_in_ref[...].T, gain_out_ref[...].T
    for i in range(rows):
        _, update, grad_gate = gate_grads(
            i, rows, factor_ref, cot_ref, gain_out, w_out, turned_ref
        )
        update_ref[i] = update.T.astype(BF16)
        grads = edge_parts(i, rows, factor_ref, left_ref, right_ref) + [grad_gate]
        grads = jnp.concatenate(grads, axis=0)
        scaled = jnp.dot(weight, grads, preferred_element_type=F32) * gain_in
        centred, inv_std = norm_rows(pair_ref[i].astype(F32).T)
        first = jnp.sum(scaled, axis=0, keepdims=True) * (1.0 / width)
        second = jnp.sum(scaled * centred, axis=0, keepdims=True) * (1.0 / width)
        grad_pair = inv_std * (scaled - first - centred * second)
        out_ref[i] = grad_pair.T.astype(BF16)


def finish_kernel(full_ref, weight_ref, w_out_ref, gain_in_ref, gain_out_ref, *outs):
    grad_weight_ref, grad_out_ref, grad_gain_in_ref, grad_gain_out_ref = outs
    width = w_out_ref.shape[0]
    full = full_ref[...].astype(F32).reshape(6 * width, width)
    weight = weight_ref[...].astype(F32)
    total = jnp.zeros((width, width), F32)
    for b in range(5):
        block = full[b * width : (b + 1) * width]
        grad_weight_ref[:, b * width : (b + 1) * width] = block
        total = total + block * weight[:, b * width : (b + 1) * width]
    block = full[5 * width :]
    grad_out_ref[...] = block
    total_out = block * w_out_ref[...].astype(F32)
    grad_gain_in_ref[...] = jnp.sum(total.T, axis=0, keepdims=True) / gain_in_ref[...]
    grad_gain_out_ref[...] = jnp.sum(total_out.T, axis=0, keepdims=True) / gain_out_ref[...]


def local(devices, pair, gain_in, w_proj, gain_out, w_out, cotangent):
    width = gain_out.shape[0]
    rows, res, _ = pair.shape
    share = width // devices
    half = share * rows
    shape = jax.ShapeDtypeStruct
    scratch = [pltpu.VMEM((res // LANES, width * rows, LANES), F32)] * 2

    sent = call(
        edges_kernel,
        shape((devices, 2 * half, res), BF16),
        (pair, gain_in[None], w_proj),
        scratch
        + [pltpu.VMEM(pair.shape, BF16), pltpu.VMEM((1, width), F32)]
        + [pltpu.VMEM(w_proj.shape, BF16), pltpu.SemaphoreType.DMA((3,))],
        outside=3,
        limit=62,
    )
    sent, pair, cotangent = hold(sent, pair, cotangent)
    got = exchange(sent)

    turned = shape((rows, width, res), BF16)
    normed, factor, grad_proj_out, scaled = call(
        prepare_kernel,
        (
            turned,
            shape((rows, 5 * width, res), F32),
            turned,
            shape((res // LANES, width * rows, LANES), F32),
        ),
        (pair, cotangent, gain_in[None], gain_out[None], w_proj, w_out),
        flops=2 * rows * res * width * 6 * width,
    )
    got, normed, factor, grad_proj_out, scaled = hold(got, normed, factor, grad_proj_out, scaled)
    edge = shape((share, devices * rows, res), BF16)
    sent, left, right = call(
        functools.partial(triangle_kernel, share, rows),
        (shape((devices, half, res), BF16), edge, edge),
        (got,),
    )
    triangle = exchange(sent)
    sent = call(
        functools.partial(norm_grad_kernel, rows),
        shape((devices, half, res), BF16),
        (triangle, scaled),
    )
    got = exchange(sent)
    sent = call(
        functools.partial(edge_grads_kernel, share, rows),
        shape((devices, 2 * half, res), BF16),
        (got, left, right),
    )
    got = exchange(sent)
    sent = call(
        weight_grads_kernel,
        shape((devices, 6 * width // devices, width), BF16),
        (got, factor, normed, triangle, cotangent, grad_proj_out, gain_out[None], w_out),
        scratch + scratch[:1],
    )
    sums = exchange(sent)
    mine = jnp.sum(sums.astype(F32), axis=0).astype(BF16)
    mine = jnp.broadcast_to(mine[None], (devices,) + mine.shape)
    mine, edge_grads, factor, triangle = hold(mine, got, factor, triangle)
    full = exchange(mine)
    grad_pair, update = call(
        pair_grad_kernel,
        [shape((rows, res, width), BF16)] * 2,
        (edge_grads, factor, pair, triangle, cotangent)
        + (gain_in[None], gain_out[None], w_proj, w_out),
        scratch + scratch[:1],
        flops=2 * rows * res * width * 6 * width,
    )
    grad_w_proj, grad_w_out, grad_gain_in, grad_gain_out = call(
        finish_kernel,
        (
            shape((width, 5 * width), F32),
            shape((width, width), F32),
            shape((1, width), F32),
            shape((1, width), F32),
        ),
        (full, w_proj, w_out, gain_in[None], gain_out[None]),
    )
    return (update, grad_pair, grad_gain_in[0], grad_w_proj, grad_gain_out[0], grad_w_out)


def solution(mesh):
    devices = mesh.shape["dap"]

    def program(*args):
        return local(devices, *args)

    in_specs = (P(("dp", "dap"), None, None), P(), P(), P(), P(), P(("dp", "dap"), None, None))
    out_specs = (
        P(("dp", "dap"), None, None),
        P(("dp", "dap"), None, None),
        P("dp"),
        P("dp", None),
        P("dp"),
        P("dp", None),
    )
    return jax.shard_map(program, mesh=mesh, in_specs=in_specs, out_specs=out_specs, check_vma=False)
```

time: 159 us -> 155 us (0.975)
  blocking collectives: 47.6 us -> 91.4 us
  waiting for transfers between devices: 50.4 us -> 19.1 us
  starting transfers between devices: 28.1 us -> 16.5 us
  other arithmetic: 6.53 us -> 0.04 us
  matrix products: 3.32 us -> 0 us
  Pallas kernels: 11.6 us -> 14.6 us
  local copies, waits for them, and re-layouts: 9.8 us -> 11.4 us
    all_to_all x2 -> x4, blocking collectives: 47.6 us -> 91.4 us  [exchange(): return lax.all_to_all(values, 'dap', 0, 0, tiled=True)]
    all_to_all x4 -> x2, waiting for transfers between devices: 50.4 us -> 19.1 us  [exchange(): return lax.all_to_all(values, 'dap', 0, 0, tiled=True)]
    all_to_all x4 -> x2, starting transfers between devices: 28.1 us -> 16.5 us  [exchange(): return lax.all_to_all(values, 'dap', 0, 0, tiled=True)]
    unnamed x27 -> x38, local copies, waits for them, and re-layouts: 4.1 us -> 10.7 us
    convert_element_type x4 -> x0, other arithmetic: 3.32 us -> none  [the longest x1 1.96 us: local(): grad_proj_out = (cot * out_gate).astype(BF16)]
    dot_general x5 -> x0, matrix products: 3.32 us -> none  [the longest x1 1.38 us: local(): jnp.einsum('hc,ihk->ick', w_out, out_normed, preferred_element_type=F32)]
    pallas_call x7 -> x8, Pallas kernels: 11.6 us -> 14.6 us  [call(): pl.pallas_call(kernel, out_shape=out_shape, in_specs=[pl.BlockSpec(memory...]
    concatenate x2 -> x0, other arithmetic: 2.22 us -> none  [the longest x1 2.21 us: local(): jnp.concatenate([left_sig, left_val * left_sig * (1.0 - left_sig), right_...]
  transfers between devices with their start and end apart: 4 -> 2, of which waited for: 4 -> 2; matrix products, arithmetic and copies ran while one was open for 9% -> 0% of each run, Pallas kernels for 3% -> 4%
where the time goes in v3:
time: 155 us; the launch traced here: 154 us
  blocking collectives  91.4 us (59%)
  waiting for transfers between devices  19.1 us (12%)
  starting transfers between devices  16.5 us (11%)
  Pallas kernels  14.6 us (9%)
  local copies, waits for them, and re-layouts  11.4 us (7%)
    all_to_all x4, blocking collectives, exchange(): return lax.all_to_all(values, 'dap', 0, 0, tiled=True)  91.4 us
    all_to_all x2, waiting for transfers between devices, exchange(): return lax.all_to_all(values, 'dap', 0, 0, tiled=True)  19.1 us
    all_to_all x2, starting transfers between devices, exchange(): return lax.all_to_all(values, 'dap', 0, 0, tiled=True)  16.5 us
    pallas_call x8, Pallas kernels, call(): pl.pallas_call(kernel, out_shape=out_shape, in_specs=[pl.BlockSpec(memory...  14.6 us
    unnamed x38, local copies, waits for them, and re-layouts  10.7 us
  transfers between devices with their start and end apart: 2, of which 2 were waited for; matrix products, arithmetic and copies ran while one was open for 0% of the time, Pallas kernels for 4%

profile of v3, /device:TPU:1, one launch (start us, length us, event | category | flops | bytes accessed | tf_op | source)
XLA Modules:
  0.0 153.9 jit_solution(9478827154842837993)
XLA Ops:
  0.6 3.3 %shard_map.109 = bf16[32,64,256]{2,1,0:T(8,128)(2,1)} custom-call(bf16[8,256,128]{2,1,0:T(8,128)(2,1)} %pair_ref.1, f32[1,128]{1,0:T(1,128)} %bitcast.4, bf16[128,640]{1,0:T(8,128)(2,1)} %weight_ref.5), custom_call_target="tpu_custom_call" | custom-call | bytes 1737216 | tf_op jit(solution)/shard_map/pallas_call | solution.py:29
  4.0 11.1 %all-to-all-start = ((bf16[32,64,256]{2,1,0:T(8,128)(2,1)}), bf16[32,64,256]{2,1,0:T(8,128)(2,1)S(1)}, u32[]{:S(2)}, u32[]{:S(2)}) async-start(bf16[32,64,256]{2,1,0:T(8,128)(2,1)} %shard_map.109), calls=%async_computation | async-start | bytes 2097152 | tf_op jit(solution)/shard_map/all_to_all | solution.py:17
  15.1 0.0 copy-start.3
  15.1 1.0 copy-done.3
  16.2 0.0 copy-start.5
  16.2 1.0 copy-done.5
  17.2 0.0 copy-start.7
  17.2 0.9 copy-done.7
  18.1 0.0 copy-start.13
  18.1 0.8 copy-done.13
  18.9 0.0 copy-start.15
  18.9 0.7 copy-done.15
  19.6 0.0 copy-start.17
  19.6 0.7 copy-done.17
  20.2 3.2 %shard_map.110 = (bf16[8,128,256]{2,1,0:T(8,128)(2,1)S(1)}, f32[8,640,256]{2,1,0:T(8,128)S(1)}, bf16[8,128,256]{2,1,0:T(8,128)(2,1)S(1)}, f32[2,1024,128]{2,1,0:T(8,128)S(1)}) custom-call(bf16[8,256,128]{2,1,0:T(8,128)(2,1)S(1)} %copy-done.5, bf16[8,256,128]{2,1,0:T(8,128)(2,1)S(1)} %copy-done.3, f32[1,128]{1,0:T(1,128)S(1)} %bitcast.5, ...), custom_call_target="tpu_custom_call" | custom-call | flops 402653184 | bytes 8586240 | tf_op jit(solution)/shard_map/pallas_call | solution.py:29
  23.5 0.0 copy-start
  23.5 2.3 %copy-done = f32[8,640,256]{2,1,0:T(8,128)} copy-done((f32[8,640,256]{2,1,0:T(8,128)}, f32[8,640,256]{2,1,0:T(8,128)S(1)}, u32[]{:S(2)}) %copy-start) | copy-done | bytes 5242904
  25.8 0.0 copy-start.9
  25.8 0.8 copy-done.9
  26.6 0.0 copy-start.11
  26.6 0.0 copy-start.4
  26.6 0.0 copy-start.14
  26.6 0.0 copy-start.18
  26.6 15.0 %all-to-all-done.got_ref = bf16[32,64,256]{2,1,0:T(8,128)(2,1)S(1)} async-done(((bf16[32,64,256]{2,1,0:T(8,128)(2,1)}), bf16[32,64,256]{2,1,0:T(8,128)(2,1)S(1)}, u32[]{:S(2)}, u32[]{:S(2)}) %all-to-all-start) | async-done | bytes 1048608 | tf_op jit(solution)/shard_map/all_to_all | solution.py:17
  41.6 0.0 copy-start.1
  41.6 0.0 copy-start.10
  41.6 0.4 shard_map.111
  42.0 0.0 copy-done.11
  42.0 0.0 copy-start.12
  42.0 22.6 %all_to_all.30.got_ref.triangle_ref = bf16[32,32,256]{2,1,0:T(8,128)(2,1)S(1)} all-to-all(bf16[32,32,256]{2,1,0:T(8,128)(2,1)S(1)} %get-tuple-element.39), channel_id=1, replica_groups=mesh['dp'=8,'dap'=32] {'dap'}, dimensions={0} | all-to-all | bytes 1048576 | tf_op jit(solution)/shard_map/all_to_all | solution.py:17
  64.6 0.6 shard_map.112
  65.2 21.5 %all_to_all.31.got_ref = bf16[32,32,256]{2,1,0:T(8,128)(2,1)S(1)} all-to-all(bf16[32,32,256]{2,1,0:T(8,128)(2,1)S(1)} %shard_map.112), channel_id=1, replica_groups=mesh['dp'=8,'dap'=32] {'dap'}, dimensions={0} | all-to-all | bytes 1048576 | tf_op jit(solution)/shard_map/all_to_all | solution.py:17
  86.7 0.5 shard_map.113
  87.2 31.2 %all_to_all.32.got_ref = bf16[32,64,256]{2,1,0:T(8,128)(2,1)S(1)} all-to-all(bf16[32,64,256]{2,1,0:T(8,128)(2,1)S(1)} %shard_map.113), channel_id=1, replica_groups=mesh['dp'=8,'dap'=32] {'dap'}, dimensions={0} | all-to-all | bytes 2097152 | tf_op jit(solution)/shard_map/all_to_all | solution.py:17
  118.4 0.0 copy-done.4
  118.4 0.0 copy-done.14
  118.4 0.0 copy-done.18
  118.4 0.0 copy-done.1
  118.4 0.0 copy-done.10
  118.4 0.0 copy-done.12
  118.4 0.0 copy-start.6
  118.4 0.0 copy-start.8
  118.4 0.0 copy-start.16
  118.5 2.1 %shard_map.114 = bf16[32,24,128]{2,1,0:T(8,128)(2,1)S(1)} custom-call(bf16[32,64,256]{2,1,0:T(8,128)(2,1)S(1)} %all_to_all.32.got_ref, f32[8,640,256]{2,1,0:T(8,128)S(1)} %copy-done.1, bf16[8,128,256]{2,1,0:T(8,128)(2,1)S(1)} %copy-done.10, bf16[32,32,256]{2,1,0:T(8,128)(2,1)S(1)} %all_to_all.30.got_ref.triangle_ref, bf16[8,256,128]{2,1,0:T(8,128)(2,1)S(1)} %copy-done.4, ...), custom_call_target="tpu_custom_call" | custom-call | bytes 8618496 | tf_op jit(solution)/shard_map/pallas_call | solution.py:29
  120.6 16.1 %all_to_all.33 = bf16[32,24,128]{2,1,0:T(8,128)(2,1)S(1)} all-to-all(bf16[32,24,128]{2,1,0:T(8,128)(2,1)S(1)} %shard_map.114), channel_id=1, replica_groups=mesh['dp'=8,'dap'=32] {'dap'}, dimensions={0} | all-to-all | bytes 393216 | tf_op jit(solution)/shard_map/all_to_all | solution.py:17
  136.7 0.7 broadcast_in_dim.8
  137.4 5.4 %all-to-all-start.5 = ((bf16[32,24,128]{2,1,0:T(8,128)(2,1)}), bf16[32,24,128]{2,1,0:T(8,128)(2,1)S(1)}, u32[]{:S(2)}, u32[]{:S(2)}) async-start(bf16[32,24,128]{2,1,0:T(8,128)(2,1)} %broadcast_in_dim.8), calls=%async_computation.5 | async-start | bytes 393216 | tf_op jit(solution)/shard_map/all_to_all | solution.py:17
  142.8 0.0 copy-done.6
  142.8 0.0 copy-done.8
  142.8 0.0 copy-done.16
  142.8 0.0 copy-start.2
  142.8 2.5 %copy-done.2 = f32[8,640,256]{2,1,0:T(8,128)S(1)} copy-done((f32[8,640,256]{2,1,0:T(8,128)S(1)}, f32[8,640,256]{2,1,0:T(8,128)}, u32[]{:S(2)}) %copy-start.2) | copy-done | bytes 5242904
  145.3 3.6 %shard_map.115 = (bf16[8,256,128]{2,1,0:T(8,128)(2,1)}, bf16[8,256,128]{2,1,0:T(8,128)(2,1)}) custom-call(bf16[32,64,256]{2,1,0:T(8,128)(2,1)S(1)} %all_to_all.32.got_ref, f32[8,640,256]{2,1,0:T(8,128)S(1)} %copy-done.2, bf16[8,256,128]{2,1,0:T(8,128)(2,1)S(1)} %copy-done.6, bf16[32,32,256]{2,1,0:T(8,128)(2,1)S(1)} %all_to_all.30.got_ref.triangle_ref, ...), custom_call_target="tpu_custom_call" | custom-call | flops 402653184 | bytes 9110528 | tf_op jit(solution)/shard_map/pallas_call | solution.py:29
  149.0 4.2 %all-to-all-done.5.full_ref = bf16[32,24,128]{2,1,0:T(8,128)(2,1)S(1)} async-done(((bf16[32,24,128]{2,1,0:T(8,128)(2,1)}), bf16[32,24,128]{2,1,0:T(8,128)(2,1)S(1)}, u32[]{:S(2)}, u32[]{:S(2)}) %all-to-all-start.5) | async-done | bytes 196640 | tf_op jit(solution)/shard_map/all_to_all | solution.py:17
  153.1 0.8 shard_map.116
  (1 shorter events, 0.0 us)
Async XLA Ops:
  4.0 37.6 %all-to-all-start = ((bf16[32,64,256]{2,1,0:T(8,128)(2,1)}), bf16[32,64,256]{2,1,0:T(8,128)(2,1)S(1)}, u32[]{:S(2)}, u32[]{:S(2)}) async-start(bf16[32,64,256]{2,1,0:T(8,128)(2,1)} %shard_map.109), calls=%async_computation | async-start | bytes 2097152 | tf_op jit(solution)/shard_map/all_to_all | solution.py:17
  15.1 1.0 copy-start.3
  16.2 1.0 copy-start.5
  17.2 0.9 copy-start.7
  18.1 0.8 copy-start.13
  18.9 0.7 copy-start.15
  19.6 0.7 copy-start.17
  23.5 2.4 %copy-start = (f32[8,640,256]{2,1,0:T(8,128)}, f32[8,640,256]{2,1,0:T(8,128)S(1)}, u32[]{:S(2)}) copy-start(f32[8,640,256]{2,1,0:T(8,128)S(1)} %get-tuple-element.47.factor_ref) | copy-start | bytes 15728644
  25.8 0.8 copy-start.9
  26.6 15.3 %copy-start.11 = (bf16[8,128,256]{2,1,0:T(8,128)(2,1)}, bf16[8,128,256]{2,1,0:T(8,128)(2,1)S(1)}, u32[]{:S(2)}) copy-start(bf16[8,128,256]{2,1,0:T(8,128)(2,1)S(1)} %get-tuple-element.45.grad_out_ref) | copy-start | bytes 1572868
  26.6 91.8 %copy-start.4 = (bf16[8,256,128]{2,1,0:T(8,128)(2,1)S(1)}, bf16[8,256,128]{2,1,0:T(8,128)(2,1)}, u32[]{:S(2)}) copy-start(bf16[8,256,128]{2,1,0:T(8,128)(2,1)} %cot_ref.2) | copy-start | bytes 1572868
  26.6 91.8 %copy-start.14 = (bf16[128,128]{1,0:T(8,128)(2,1)S(1)}, bf16[128,128]{1,0:T(8,128)(2,1)}, u32[]{:S(2)}) copy-start(bf16[128,128]{1,0:T(8,128)(2,1)} %w_out_ref.7) | copy-start | bytes 98308
  26.6 91.8 %copy-start.18 = (f32[128]{0:T(128)S(1)}, f32[128]{0:T(128)}, u32[]{:S(2)}) copy-start(f32[128]{0:T(128)} %param.9) | copy-start | bytes 1540
  41.6 76.8 %copy-start.1 = (f32[8,640,256]{2,1,0:T(8,128)S(1)}, f32[8,640,256]{2,1,0:T(8,128)}, u32[]{:S(2)}) copy-start(f32[8,640,256]{2,1,0:T(8,128)} %copy-done) | copy-start | bytes 15728644
  41.6 76.8 %copy-start.10 = (bf16[8,128,256]{2,1,0:T(8,128)(2,1)S(1)}, bf16[8,128,256]{2,1,0:T(8,128)(2,1)}, u32[]{:S(2)}) copy-start(bf16[8,128,256]{2,1,0:T(8,128)(2,1)} %copy-done.9) | copy-start | bytes 1572868
  42.0 76.4 %copy-start.12 = (bf16[8,128,256]{2,1,0:T(8,128)(2,1)S(1)}, bf16[8,128,256]{2,1,0:T(8,128)(2,1)}, u32[]{:S(2)}) copy-start(bf16[8,128,256]{2,1,0:T(8,128)(2,1)} %copy-done.11) | copy-start | bytes 1572868
  118.4 24.4 %copy-start.6 = (bf16[8,256,128]{2,1,0:T(8,128)(2,1)S(1)}, bf16[8,256,128]{2,1,0:T(8,128)(2,1)}, u32[]{:S(2)}) copy-start(bf16[8,256,128]{2,1,0:T(8,128)(2,1)} %pair_ref.1) | copy-start | bytes 1572868
  118.4 24.4 %copy-start.8 = (bf16[128,640]{1,0:T(8,128)(2,1)S(1)}, bf16[128,640]{1,0:T(8,128)(2,1)}, u32[]{:S(2)}) copy-start(bf16[128,640]{1,0:T(8,128)(2,1)} %weight_ref.5) | copy-start | bytes 491524
  118.4 24.4 %copy-start.16 = (f32[128]{0:T(128)S(1)}, f32[128]{0:T(128)}, u32[]{:S(2)}) copy-start(f32[128]{0:T(128)} %param.7) | copy-start | bytes 1540
  137.4 15.7 %all-to-all-start.5 = ((bf16[32,24,128]{2,1,0:T(8,128)(2,1)}), bf16[32,24,128]{2,1,0:T(8,128)(2,1)S(1)}, u32[]{:S(2)}, u32[]{:S(2)}) async-start(bf16[32,24,128]{2,1,0:T(8,128)(2,1)} %broadcast_in_dim.8), calls=%async_computation.5 | async-start | bytes 393216 | tf_op jit(solution)/shard_map/all_to_all | solution.py:17
  142.8 2.5 %copy-start.2 = (f32[8,640,256]{2,1,0:T(8,128)S(1)}, f32[8,640,256]{2,1,0:T(8,128)}, u32[]{:S(2)}) copy-start(f32[8,640,256]{2,1,0:T(8,128)} %copy-done) | copy-start | bytes 15728644

commit v4 on v3

--- a/solution.py
+++ b/solution.py
@@ -13,8 +13,19 @@
 NT = (((1,), (1,)), ((), ()))
 
 
+def places(devices):
+    if devices % 16:
+        return list(range(devices))
+    order = []
+    for high in range(0, devices, 16):
+        for core in range(2):
+            order += [high + 2 * z + core for z in (0, 2, 4, 6, 1, 3, 5, 7)]
+    return order
+
+
 def exchange(values):
-    return lax.all_to_all(values, "dap", 0, 0, tiled=True)
+    groups = [places(values.shape[0])]
+    return lax.all_to_all(values, "dap", 0, 0, tiled=True, axis_index_groups=groups)
 
 
 def hold(*values):
@@ -132,16 +143,25 @@
         put_row(scaled_ref, i, rows, scaled)
 
 
-def matrices_of(ref, first, share, rows):
+def reorder(block, order):
+    return jnp.stack([block[m] for m in order], axis=0)
+
+
+def matrices_of(ref, first, share, rows, in_order=False):
     devices, _, res = ref.shape
     block = ref[:, first : first + share * rows, :].astype(F32)
+    if in_order:
+        order = places(devices)
+        block = reorder(block, [order.index(d) for d in range(devices)])
     block = block.reshape(devices, share, rows, res)
     return [block[:, c].reshape(devices * rows, res).astype(BF16) for c in range(share)]
 
 
-def store_matrices(ref, first, values, rows):
+def store_matrices(ref, first, values, rows, in_order=False):
     devices, _, res = ref.shape
     block = jnp.stack([v.reshape(devices, rows, res) for v in values], axis=1)
+    if in_order:
+        block = reorder(block, places(devices))
     ref[:, first : first + len(values) * rows, :] = block.reshape(
         devices, len(values) * rows, res
     ).astype(BF16)
@@ -150,7 +170,7 @@
 def triangle_kernel(share, rows, got_ref, sent_ref, left_ref, right_ref):
     half = share * rows
     left = matrices_of(got_ref, 0, share, rows)
-    right = matrices_of(got_ref, half, share, rows)
+    right = matrices_of(got_ref, half, share, rows, in_order=True)
     for c in range(share):
         left_ref[c] = left[c]
         right_ref[c] = right[c]
@@ -207,7 +227,7 @@
         turned = grads[c].astype(F32).T.astype(BF16)
         right_grads.append(jnp.dot(turned, left_ref[c], preferred_element_type=F32))
     store_matrices(sent_ref, 0, left_grads, rows)
-    store_matrices(sent_ref, share * rows, right_grads, rows)
+    store_matrices(sent_ref, share * rows, right_grads, rows, in_order=True)
 
 
 def turn(triangle_ref, turned_ref):

time: 155 us -> 151 us (0.974)
  blocking collectives: 91.4 us -> 89.1 us
    all_to_all x4, blocking collectives: 91.4 us -> 89.1 us  [exchange(): lax.all_to_all(values, 'dap', 0, 0, tiled=True, axis_index_groups=groups)]
  transfers between devices with their start and end apart: 2 -> 2, of which waited for: 2 -> 2; matrix products, arithmetic and copies ran while one was open for 0% -> 0% of each run, Pallas kernels for 4% -> 5%
where the time goes in v4:
time: 151 us
  blocking collectives  89.1 us (59%)
  waiting for transfers between devices  18.7 us (12%)
  starting transfers between devices  15.9 us (11%)
  Pallas kernels  14.6 us (10%)
  local copies, waits for them, and re-layouts  11.4 us (8%)
    all_to_all x4, blocking collectives, exchange(): lax.all_to_all(values, 'dap', 0, 0, tiled=True, axis_index_groups=groups)  89.1 us
    all_to_all x2, waiting for transfers between devices, exchange(): lax.all_to_all(values, 'dap', 0, 0, tiled=True, axis_index_groups=groups)  18.7 us
    all_to_all x2, starting transfers between devices, exchange(): lax.all_to_all(values, 'dap', 0, 0, tiled=True, axis_index_groups=groups)  15.9 us
    pallas_call x8, Pallas kernels, call(): pl.pallas_call(kernel, out_shape=out_shape, in_specs=[pl.BlockSpec(memory...  14.6 us
    unnamed x38, local copies, waits for them, and re-layouts  10.7 us
  transfers between devices with their start and end apart: 2, of which 2 were waited for; matrix products, arithmetic and copies ran while one was open for 0% of the time, Pallas kernels for 5%

profile of v4, /device:TPU:1, one launch (start us, length us, event | category | flops | bytes accessed | tf_op | source)
XLA Modules:
  0.0 150.5 jit_solution(11946844417460344733)
XLA Ops:
  0.6 3.3 %shard_map.109 = bf16[32,64,256]{2,1,0:T(8,128)(2,1)} custom-call(bf16[8,256,128]{2,1,0:T(8,128)(2,1)} %pair_ref.1, f32[1,128]{1,0:T(1,128)} %bitcast.4, bf16[128,640]{1,0:T(8,128)(2,1)} %weight_ref.5), custom_call_target="tpu_custom_call" | custom-call | bytes 1737216 | tf_op jit(solution)/shard_map/pallas_call | solution.py:40
  4.0 11.1 %all-to-all-start = ((bf16[32,64,256]{2,1,0:T(8,128)(2,1)}), bf16[32,64,256]{2,1,0:T(8,128)(2,1)S(1)}, u32[]{:S(2)}, u32[]{:S(2)}) async-start(bf16[32,64,256]{2,1,0:T(8,128)(2,1)} %shard_map.109), calls=%async_computation | async-start | bytes 2097152 | tf_op jit(solution)/shard_map/all_to_all | solution.py:28
  15.1 0.0 copy-start.3
  15.1 1.0 copy-done.3
  16.2 0.0 copy-start.5
  16.2 1.0 copy-done.5
  17.2 0.0 copy-start.7
  17.2 0.9 copy-done.7
  18.1 0.0 copy-start.13
  18.1 0.8 copy-done.13
  18.9 0.0 copy-start.15
  18.9 0.7 copy-done.15
  19.6 0.0 copy-start.17
  19.6 0.7 copy-done.17
  20.2 3.2 %shard_map.110 = (bf16[8,128,256]{2,1,0:T(8,128)(2,1)S(1)}, f32[8,640,256]{2,1,0:T(8,128)S(1)}, bf16[8,128,256]{2,1,0:T(8,128)(2,1)S(1)}, f32[2,1024,128]{2,1,0:T(8,128)S(1)}) custom-call(bf16[8,256,128]{2,1,0:T(8,128)(2,1)S(1)} %copy-done.5, bf16[8,256,128]{2,1,0:T(8,128)(2,1)S(1)} %copy-done.3, f32[1,128]{1,0:T(1,128)S(1)} %bitcast.5, ...), custom_call_target="tpu_custom_call" | custom-call | flops 402653184 | bytes 8586240 | tf_op jit(solution)/shard_map/pallas_call | solution.py:40
  23.5 0.0 copy-start
  23.5 2.3 %copy-done = f32[8,640,256]{2,1,0:T(8,128)} copy-done((f32[8,640,256]{2,1,0:T(8,128)}, f32[8,640,256]{2,1,0:T(8,128)S(1)}, u32[]{:S(2)}) %copy-start) | copy-done | bytes 5242904
  25.8 0.0 copy-start.9
  25.8 0.8 copy-done.9
  26.6 0.0 copy-start.11
  26.6 0.0 copy-start.4
  26.6 0.0 copy-start.14
  26.6 0.0 copy-start.18
  26.6 15.4 %all-to-all-done.got_ref = bf16[32,64,256]{2,1,0:T(8,128)(2,1)S(1)} async-done(((bf16[32,64,256]{2,1,0:T(8,128)(2,1)}), bf16[32,64,256]{2,1,0:T(8,128)(2,1)S(1)}, u32[]{:S(2)}, u32[]{:S(2)}) %all-to-all-start) | async-done | bytes 1048608 | tf_op jit(solution)/shard_map/all_to_all | solution.py:28
  42.1 0.0 copy-start.1
  42.1 0.0 copy-start.10
  42.1 0.4 shard_map.111
  42.4 0.0 copy-done.11
  42.4 0.0 copy-start.12
  42.4 21.7 %all_to_all.30.got_ref.triangle_ref = bf16[32,32,256]{2,1,0:T(8,128)(2,1)S(1)} all-to-all(bf16[32,32,256]{2,1,0:T(8,128)(2,1)S(1)} %get-tuple-element.39), channel_id=1, replica_groups={{0,4,8,12,2,6,10,14,1,5,9,13,3,7,11,15,16,20,24,28,18,22,26,30,17,21,25..., dimensions={0} | all-to-all | bytes 1048576 | tf_op jit(solution)/shard_map/all_to_all | solution.py:28
  64.2 0.6 shard_map.112
  64.7 21.0 %all_to_all.31.got_ref = bf16[32,32,256]{2,1,0:T(8,128)(2,1)S(1)} all-to-all(bf16[32,32,256]{2,1,0:T(8,128)(2,1)S(1)} %shard_map.112), channel_id=1, replica_groups={{0,4,8,12,2,6,10,14,1,5,9,13,3,7,11,15,16,20,24,28,18,22,26,30,17,21,25..., dimensions={0} | all-to-all | bytes 1048576 | tf_op jit(solution)/shard_map/all_to_all | solution.py:28
  85.7 0.5 shard_map.113
  86.2 31.7 %all_to_all.32.got_ref = bf16[32,64,256]{2,1,0:T(8,128)(2,1)S(1)} all-to-all(bf16[32,64,256]{2,1,0:T(8,128)(2,1)S(1)} %shard_map.113), channel_id=1, replica_groups={{0,4,8,12,2,6,10,14,1,5,9,13,3,7,11,15,16,20,24,28,18,22,26,30,17,21,25..., dimensions={0} | all-to-all | bytes 2097152 | tf_op jit(solution)/shard_map/all_to_all | solution.py:28
  117.9 0.0 copy-done.4
  117.9 0.0 copy-done.14
  117.9 0.0 copy-done.18
  117.9 0.0 copy-done.1
  117.9 0.0 copy-done.10
  118.0 0.0 copy-done.12
  118.0 0.0 copy-start.6
  118.0 0.0 copy-start.8
  118.0 0.0 copy-start.16
  118.0 2.1 %shard_map.114 = bf16[32,24,128]{2,1,0:T(8,128)(2,1)S(1)} custom-call(bf16[32,64,256]{2,1,0:T(8,128)(2,1)S(1)} %all_to_all.32.got_ref, f32[8,640,256]{2,1,0:T(8,128)S(1)} %copy-done.1, bf16[8,128,256]{2,1,0:T(8,128)(2,1)S(1)} %copy-done.10, bf16[32,32,256]{2,1,0:T(8,128)(2,1)S(1)} %all_to_all.30.got_ref.triangle_ref, bf16[8,256,128]{2,1,0:T(8,128)(2,1)S(1)} %copy-done.4, ...), custom_call_target="tpu_custom_call" | custom-call | bytes 8618496 | tf_op jit(solution)/shard_map/pallas_call | solution.py:40
  120.1 14.7 %all_to_all.33 = bf16[32,24,128]{2,1,0:T(8,128)(2,1)S(1)} all-to-all(bf16[32,24,128]{2,1,0:T(8,128)(2,1)S(1)} %shard_map.114), channel_id=1, replica_groups={{0,4,8,12,2,6,10,14,1,5,9,13,3,7,11,15,16,20,24,28,18,22,26,30,17,21,25..., dimensions={0} | all-to-all | bytes 393216 | tf_op jit(solution)/shard_map/all_to_all | solution.py:28
  134.8 0.7 broadcast_in_dim.8
  135.5 4.8 %all-to-all-start.5 = ((bf16[32,24,128]{2,1,0:T(8,128)(2,1)}), bf16[32,24,128]{2,1,0:T(8,128)(2,1)S(1)}, u32[]{:S(2)}, u32[]{:S(2)}) async-start(bf16[32,24,128]{2,1,0:T(8,128)(2,1)} %broadcast_in_dim.8), calls=%async_computation.5 | async-start | bytes 393216 | tf_op jit(solution)/shard_map/all_to_all | solution.py:28
  140.3 0.0 copy-done.6
  140.4 0.0 copy-done.8
  140.4 0.0 copy-done.16
  140.4 0.0 copy-start.2
  140.4 2.5 %copy-done.2 = f32[8,640,256]{2,1,0:T(8,128)S(1)} copy-done((f32[8,640,256]{2,1,0:T(8,128)S(1)}, f32[8,640,256]{2,1,0:T(8,128)}, u32[]{:S(2)}) %copy-start.2) | copy-done | bytes 5242904
  142.9 3.6 %shard_map.115 = (bf16[8,256,128]{2,1,0:T(8,128)(2,1)}, bf16[8,256,128]{2,1,0:T(8,128)(2,1)}) custom-call(bf16[32,64,256]{2,1,0:T(8,128)(2,1)S(1)} %all_to_all.32.got_ref, f32[8,640,256]{2,1,0:T(8,128)S(1)} %copy-done.2, bf16[8,256,128]{2,1,0:T(8,128)(2,1)S(1)} %copy-done.6, bf16[32,32,256]{2,1,0:T(8,128)(2,1)S(1)} %all_to_all.30.got_ref.triangle_ref, ...), custom_call_target="tpu_custom_call" | custom-call | flops 402653184 | bytes 9110528 | tf_op jit(solution)/shard_map/pallas_call | solution.py:40
  146.5 3.2 %all-to-all-done.5.full_ref = bf16[32,24,128]{2,1,0:T(8,128)(2,1)S(1)} async-done(((bf16[32,24,128]{2,1,0:T(8,128)(2,1)}), bf16[32,24,128]{2,1,0:T(8,128)(2,1)S(1)}, u32[]{:S(2)}, u32[]{:S(2)}) %all-to-all-start.5) | async-done | bytes 196640 | tf_op jit(solution)/shard_map/all_to_all | solution.py:28
  149.7 0.8 shard_map.116
  (1 shorter events, 0.0 us)
Async XLA Ops:
  4.0 38.1 %all-to-all-start = ((bf16[32,64,256]{2,1,0:T(8,128)(2,1)}), bf16[32,64,256]{2,1,0:T(8,128)(2,1)S(1)}, u32[]{:S(2)}, u32[]{:S(2)}) async-start(bf16[32,64,256]{2,1,0:T(8,128)(2,1)} %shard_map.109), calls=%async_computation | async-start | bytes 2097152 | tf_op jit(solution)/shard_map/all_to_all | solution.py:28
  15.1 1.0 copy-start.3
  16.2 1.0 copy-start.5
  17.2 0.9 copy-start.7
  18.1 0.8 copy-start.13
  18.9 0.7 copy-start.15
  19.6 0.7 copy-start.17
  23.5 2.4 %copy-start = (f32[8,640,256]{2,1,0:T(8,128)}, f32[8,640,256]{2,1,0:T(8,128)S(1)}, u32[]{:S(2)}) copy-start(f32[8,640,256]{2,1,0:T(8,128)S(1)} %get-tuple-element.47.factor_ref) | copy-start | bytes 15728644
  25.8 0.8 copy-start.9
  26.6 15.8 %copy-start.11 = (bf16[8,128,256]{2,1,0:T(8,128)(2,1)}, bf16[8,128,256]{2,1,0:T(8,128)(2,1)S(1)}, u32[]{:S(2)}) copy-start(bf16[8,128,256]{2,1,0:T(8,128)(2,1)S(1)} %get-tuple-element.45.grad_out_ref) | copy-start | bytes 1572868
  26.6 91.3 %copy-start.4 = (bf16[8,256,128]{2,1,0:T(8,128)(2,1)S(1)}, bf16[8,256,128]{2,1,0:T(8,128)(2,1)}, u32[]{:S(2)}) copy-start(bf16[8,256,128]{2,1,0:T(8,128)(2,1)} %cot_ref.2) | copy-start | bytes 1572868
  26.6 91.3 %copy-start.14 = (bf16[128,128]{1,0:T(8,128)(2,1)S(1)}, bf16[128,128]{1,0:T(8,128)(2,1)}, u32[]{:S(2)}) copy-start(bf16[128,128]{1,0:T(8,128)(2,1)} %w_out_ref.7) | copy-start | bytes 98308
  26.6 91.3 %copy-start.18 = (f32[128]{0:T(128)S(1)}, f32[128]{0:T(128)}, u32[]{:S(2)}) copy-start(f32[128]{0:T(128)} %param.9) | copy-start | bytes 1540
  42.1 75.9 %copy-start.1 = (f32[8,640,256]{2,1,0:T(8,128)S(1)}, f32[8,640,256]{2,1,0:T(8,128)}, u32[]{:S(2)}) copy-start(f32[8,640,256]{2,1,0:T(8,128)} %copy-done) | copy-start | bytes 15728644
  42.1 75.9 %copy-start.10 = (bf16[8,128,256]{2,1,0:T(8,128)(2,1)S(1)}, bf16[8,128,256]{2,1,0:T(8,128)(2,1)}, u32[]{:S(2)}) copy-start(bf16[8,128,256]{2,1,0:T(8,128)(2,1)} %copy-done.9) | copy-start | bytes 1572868
  42.4 75.5 %copy-start.12 = (bf16[8,128,256]{2,1,0:T(8,128)(2,1)S(1)}, bf16[8,128,256]{2,1,0:T(8,128)(2,1)}, u32[]{:S(2)}) copy-start(bf16[8,128,256]{2,1,0:T(8,128)(2,1)} %copy-done.11) | copy-start | bytes 1572868
  118.0 22.4 %copy-start.6 = (bf16[8,256,128]{2,1,0:T(8,128)(2,1)S(1)}, bf16[8,256,128]{2,1,0:T(8,128)(2,1)}, u32[]{:S(2)}) copy-start(bf16[8,256,128]{2,1,0:T(8,128)(2,1)} %pair_ref.1) | copy-start | bytes 1572868
  118.0 22.4 %copy-start.8 = (bf16[128,640]{1,0:T(8,128)(2,1)S(1)}, bf16[128,640]{1,0:T(8,128)(2,1)}, u32[]{:S(2)}) copy-start(bf16[128,640]{1,0:T(8,128)(2,1)} %weight_ref.5) | copy-start | bytes 491524
  118.0 22.4 %copy-start.16 = (f32[128]{0:T(128)S(1)}, f32[128]{0:T(128)}, u32[]{:S(2)}) copy-start(f32[128]{0:T(128)} %param.7) | copy-start | bytes 1540
  135.5 14.2 %all-to-all-start.5 = ((bf16[32,24,128]{2,1,0:T(8,128)(2,1)}), bf16[32,24,128]{2,1,0:T(8,128)(2,1)S(1)}, u32[]{:S(2)}, u32[]{:S(2)}) async-start(bf16[32,24,128]{2,1,0:T(8,128)(2,1)} %broadcast_in_dim.8), calls=%async_computation.5 | async-start | bytes 393216 | tf_op jit(solution)/shard_map/all_to_all | solution.py:28
  140.4 2.5 %copy-start.2 = (f32[8,640,256]{2,1,0:T(8,128)S(1)}, f32[8,640,256]{2,1,0:T(8,128)}, u32[]{:S(2)}) copy-start(f32[8,640,256]{2,1,0:T(8,128)} %copy-done) | copy-start | bytes 15728644

commit v5 on v4

--- a/solution.py
+++ b/solution.py
@@ -10,6 +10,7 @@
 F32, BF16 = jnp.float32, jnp.bfloat16
 EPS = 1e-05
 LANES = 128
+PIECES = 4
 NT = (((1,), (1,)), ((), ()))
 
 
@@ -17,9 +18,9 @@
     if devices % 16:
         return list(range(devices))
     order = []
-    for high in range(0, devices, 16):
-        for core in range(2):
-            order += [high + 2 * z + core for z in (0, 2, 4, 6, 1, 3, 5, 7)]
+    for n, high in enumerate(range(0, devices, 16)):
+        for core in (n % 2, 1 - n % 2):
+            order += [high + 2 * z + core for z in (0, 3, 4, 7, 1, 2, 5, 6)]
     return order
 
 
@@ -32,11 +33,14 @@
     return lax.optimization_barrier(values)
 
 
-def call(kernel, out_shape, operands, scratch=(), flops=0, outside=0, limit=16):
+def call(kernel, out_shape, operands, scratch=(), flops=0, outside=0, limit=16, leave=False):
     leaves = out_shape if isinstance(out_shape, (tuple, list)) else [out_shape]
     moved = sum(a.size * a.dtype.itemsize for a in list(operands) + list(leaves))
     spec = pl.BlockSpec(memory_space=pltpu.VMEM)
-    out_specs = [spec] * len(out_shape) if isinstance(out_shape, (tuple, list)) else spec
+    if leave:
+        out_specs = pl.BlockSpec(memory_space=pl.ANY)
+    else:
+        out_specs = [spec] * len(out_shape) if isinstance(out_shape, (tuple, list)) else spec
     return pl.pallas_call(
         kernel,
         out_shape=out_shape,
@@ -77,7 +81,7 @@
 
 
 def edges_kernel(
-    pair_hbm, gain_hbm, weight_hbm, sent_ref, left_ref, right_ref, pair_ref, gain_ref, weight_ref, sems
+    pair_hbm, gain_hbm, weight_hbm, sent_hbm, left_ref, right_ref, pair_ref, gain_ref, weight_ref, sent_ref, sems
 ):
     rows, res, width = pair_ref.shape
     devices = sent_ref.shape[0]
@@ -95,15 +99,25 @@
     gain = gain_ref[...].T
     copies[2].wait()
     for i in range(rows):
-        centred, _ = norm_rows(pair_ref[i].astype(F32).T)
+        centred, _ = norm_rows(pair_ref[i].T.astype(F32))
         normed = (centred * gain).astype(BF16)
         out = jnp.dot(weight, normed, preferred_element_type=F32)
         put_row(left_ref, i, rows, jax.nn.sigmoid(out[width : 2 * width]) * out[:width])
         put_row(right_ref, i, rows, jax.nn.sigmoid(out[3 * width :]) * out[2 * width : 3 * width])
-    for n, ref in enumerate((left_ref, right_ref)):
-        for h in range(res // LANES):
-            block = ref[h].reshape(devices, half, LANES).astype(BF16)
-            sent_ref[:, n * half : (n + 1) * half, h * LANES : (h + 1) * LANES] = block
+    step = devices // PIECES
+    copies = []
+    for piece in range(PIECES):
+        slots = pl.ds(piece * step, step)
+        for n, ref in enumerate((left_ref, right_ref)):
+            for h in range(res // LANES):
+                block = ref[h, pl.ds(piece * step * half, step * half), :]
+                block = block.reshape(step, half, LANES).astype(BF16)
+                sent_ref[slots, n * half : (n + 1) * half, h * LANES : (h + 1) * LANES] = block
+        copy = pltpu.make_async_copy(sent_ref.at[slots], sent_hbm.at[slots], sems.at[3 + piece])
+        copy.start()
+        copies.append(copy)
+    for copy in copies:
+        copy.wait()
 
 
 def prepare_kernel(
@@ -355,8 +369,10 @@
         (pair, gain_in[None], w_proj),
         scratch
         + [pltpu.VMEM(pair.shape, BF16), pltpu.VMEM((1, width), F32)]
-        + [pltpu.VMEM(w_proj.shape, BF16), pltpu.SemaphoreType.DMA((3,))],
+        + [pltpu.VMEM(w_proj.shape, BF16), pltpu.VMEM((devices, 2 * half, res), BF16)]
+        + [pltpu.SemaphoreType.DMA((3 + PIECES,))],
         outside=3,
+        leave=True,
         limit=62,
     )
     sent, pair, cotangent = hold(sent, pair, cotangent)

time: 151 us -> 150 us (level)
  waiting for transfers between devices: 18.7 us -> 16.2 us
    all_to_all x2, waiting for transfers between devices: 18.7 us -> 16.2 us  [exchange(): lax.all_to_all(values, 'dap', 0, 0, tiled=True, axis_index_groups=groups)]
where the time goes in v5:
time: 150 us
  blocking collectives  90.2 us (60%)
  starting transfers between devices  16.5 us (11%)
  waiting for transfers between devices  16.2 us (11%)
  Pallas kernels  14.4 us (10%)
  local copies, waits for them, and re-layouts  11.4 us (8%)
    all_to_all x4, blocking collectives, exchange(): lax.all_to_all(values, 'dap', 0, 0, tiled=True, axis_index_groups=groups)  90.2 us
    all_to_all x2, starting transfers between devices, exchange(): lax.all_to_all(values, 'dap', 0, 0, tiled=True, axis_index_groups=groups)  16.5 us
    all_to_all x2, waiting for transfers between devices, exchange(): lax.all_to_all(values, 'dap', 0, 0, tiled=True, axis_index_groups=groups)  16.2 us
    pallas_call x8, Pallas kernels, call(): pl.pallas_call(kernel, out_shape=out_shape, in_specs=[pl.BlockSpec(memory...  14.4 us
    unnamed x38, local copies, waits for them, and re-layouts  10.7 us
  transfers between devices with their start and end apart: 2, of which 2 were waited for; matrix products, arithmetic and copies ran while one was open for 0% of the time, Pallas kernels for 5%

profile of v5, /device:TPU:1, one launch (start us, length us, event | category | flops | bytes accessed | tf_op | source)
XLA Modules:
  0.0 149.7 jit_solution(13376832343804111893)
XLA Ops:
  0.6 3.2 %shard_map.109 = bf16[32,64,256]{2,1,0:T(8,128)(2,1)} custom-call(bf16[8,256,128]{2,1,0:T(8,128)(2,1)} %pair_ref.1, f32[1,128]{1,0:T(1,128)} %bitcast.4, bf16[128,640]{1,0:T(8,128)(2,1)} %weight_ref.5), custom_call_target="tpu_custom_call" | custom-call | bytes 1737216 | tf_op jit(solution)/shard_map/pallas_call | solution.py:44
  3.8 11.2 %all-to-all-start = ((bf16[32,64,256]{2,1,0:T(8,128)(2,1)}), bf16[32,64,256]{2,1,0:T(8,128)(2,1)S(1)}, u32[]{:S(2)}, u32[]{:S(2)}) async-start(bf16[32,64,256]{2,1,0:T(8,128)(2,1)} %shard_map.109), calls=%async_computation | async-start | bytes 2097152 | tf_op jit(solution)/shard_map/all_to_all | solution.py:29
  15.0 0.0 copy-start.3
  15.0 1.0 copy-done.3
  16.1 0.0 copy-start.5
  16.1 1.0 copy-done.5
  17.1 0.0 copy-start.7
  17.1 0.9 copy-done.7
  18.0 0.0 copy-start.13
  18.0 0.8 copy-done.13
  18.8 0.0 copy-start.15
  18.8 0.7 copy-done.15
  19.4 0.0 copy-start.17
  19.4 0.7 copy-done.17
  20.1 3.2 %shard_map.110 = (bf16[8,128,256]{2,1,0:T(8,128)(2,1)S(1)}, f32[8,640,256]{2,1,0:T(8,128)S(1)}, bf16[8,128,256]{2,1,0:T(8,128)(2,1)S(1)}, f32[2,1024,128]{2,1,0:T(8,128)S(1)}) custom-call(bf16[8,256,128]{2,1,0:T(8,128)(2,1)S(1)} %copy-done.5, bf16[8,256,128]{2,1,0:T(8,128)(2,1)S(1)} %copy-done.3, f32[1,128]{1,0:T(1,128)S(1)} %bitcast.5, ...), custom_call_target="tpu_custom_call" | custom-call | flops 402653184 | bytes 8586240 | tf_op jit(solution)/shard_map/pallas_call | solution.py:44
  23.3 0.0 copy-start
  23.3 2.3 %copy-done = f32[8,640,256]{2,1,0:T(8,128)} copy-done((f32[8,640,256]{2,1,0:T(8,128)}, f32[8,640,256]{2,1,0:T(8,128)S(1)}, u32[]{:S(2)}) %copy-start) | copy-done | bytes 5242904
  25.7 0.0 copy-start.9
  25.7 0.8 copy-done.9
  26.5 0.0 copy-start.11
  26.5 0.0 copy-start.4
  26.5 0.0 copy-start.14
  26.5 0.0 copy-start.18
  26.5 13.6 %all-to-all-done.got_ref = bf16[32,64,256]{2,1,0:T(8,128)(2,1)S(1)} async-done(((bf16[32,64,256]{2,1,0:T(8,128)(2,1)}), bf16[32,64,256]{2,1,0:T(8,128)(2,1)S(1)}, u32[]{:S(2)}, u32[]{:S(2)}) %all-to-all-start) | async-done | bytes 1048608 | tf_op jit(solution)/shard_map/all_to_all | solution.py:29
  40.1 0.0 copy-start.1
  40.1 0.0 copy-start.10
  40.1 0.4 shard_map.111
  40.5 0.0 copy-done.11
  40.5 0.0 copy-start.12
  40.5 21.3 %all_to_all.30.got_ref.triangle_ref = bf16[32,32,256]{2,1,0:T(8,128)(2,1)S(1)} all-to-all(bf16[32,32,256]{2,1,0:T(8,128)(2,1)S(1)} %get-tuple-element.39), channel_id=1, replica_groups={{0,6,8,14,2,4,10,12,1,7,9,15,3,5,11,13,17,23,25,31,19,21,27,29,16,22,24..., dimensions={0} | all-to-all | bytes 1048576 | tf_op jit(solution)/shard_map/all_to_all | solution.py:29
  61.8 0.6 shard_map.112
  62.4 21.0 %all_to_all.31.got_ref = bf16[32,32,256]{2,1,0:T(8,128)(2,1)S(1)} all-to-all(bf16[32,32,256]{2,1,0:T(8,128)(2,1)S(1)} %shard_map.112), channel_id=1, replica_groups={{0,6,8,14,2,4,10,12,1,7,9,15,3,5,11,13,17,23,25,31,19,21,27,29,16,22,24..., dimensions={0} | all-to-all | bytes 1048576 | tf_op jit(solution)/shard_map/all_to_all | solution.py:29
  83.3 0.5 shard_map.113
  83.8 32.1 %all_to_all.32.got_ref = bf16[32,64,256]{2,1,0:T(8,128)(2,1)S(1)} all-to-all(bf16[32,64,256]{2,1,0:T(8,128)(2,1)S(1)} %shard_map.113), channel_id=1, replica_groups={{0,6,8,14,2,4,10,12,1,7,9,15,3,5,11,13,17,23,25,31,19,21,27,29,16,22,24..., dimensions={0} | all-to-all | bytes 2097152 | tf_op jit(solution)/shard_map/all_to_all | solution.py:29
  115.9 0.0 copy-done.4
  115.9 0.0 copy-done.14
  115.9 0.0 copy-done.18
  115.9 0.0 copy-done.1
  115.9 0.0 copy-done.10
  116.0 0.0 copy-done.12
  116.0 0.0 copy-start.6
  116.0 0.0 copy-start.8
  116.0 0.0 copy-start.16
  116.0 2.1 %shard_map.114 = bf16[32,24,128]{2,1,0:T(8,128)(2,1)S(1)} custom-call(bf16[32,64,256]{2,1,0:T(8,128)(2,1)S(1)} %all_to_all.32.got_ref, f32[8,640,256]{2,1,0:T(8,128)S(1)} %copy-done.1, bf16[8,128,256]{2,1,0:T(8,128)(2,1)S(1)} %copy-done.10, bf16[32,32,256]{2,1,0:T(8,128)(2,1)S(1)} %all_to_all.30.got_ref.triangle_ref, bf16[8,256,128]{2,1,0:T(8,128)(2,1)S(1)} %copy-done.4, ...), custom_call_target="tpu_custom_call" | custom-call | bytes 8618496 | tf_op jit(solution)/shard_map/pallas_call | solution.py:44
  118.1 15.9 %all_to_all.33 = bf16[32,24,128]{2,1,0:T(8,128)(2,1)S(1)} all-to-all(bf16[32,24,128]{2,1,0:T(8,128)(2,1)S(1)} %shard_map.114), channel_id=1, replica_groups={{0,6,8,14,2,4,10,12,1,7,9,15,3,5,11,13,17,23,25,31,19,21,27,29,16,22,24..., dimensions={0} | all-to-all | bytes 393216 | tf_op jit(solution)/shard_map/all_to_all | solution.py:29
  134.0 0.7 broadcast_in_dim.8
  134.7 5.4 %all-to-all-start.5 = ((bf16[32,24,128]{2,1,0:T(8,128)(2,1)}), bf16[32,24,128]{2,1,0:T(8,128)(2,1)S(1)}, u32[]{:S(2)}, u32[]{:S(2)}) async-start(bf16[32,24,128]{2,1,0:T(8,128)(2,1)} %broadcast_in_dim.8), calls=%async_computation.5 | async-start | bytes 393216 | tf_op jit(solution)/shard_map/all_to_all | solution.py:29
  140.1 0.0 copy-done.6
  140.1 0.0 copy-done.8
  140.1 0.0 copy-done.16
  140.1 0.0 copy-start.2
  140.1 2.5 %copy-done.2 = f32[8,640,256]{2,1,0:T(8,128)S(1)} copy-done((f32[8,640,256]{2,1,0:T(8,128)S(1)}, f32[8,640,256]{2,1,0:T(8,128)}, u32[]{:S(2)}) %copy-start.2) | copy-done | bytes 5242904
  142.6 3.6 %shard_map.115 = (bf16[8,256,128]{2,1,0:T(8,128)(2,1)}, bf16[8,256,128]{2,1,0:T(8,128)(2,1)}) custom-call(bf16[32,64,256]{2,1,0:T(8,128)(2,1)S(1)} %all_to_all.32.got_ref, f32[8,640,256]{2,1,0:T(8,128)S(1)} %copy-done.2, bf16[8,256,128]{2,1,0:T(8,128)(2,1)S(1)} %copy-done.6, bf16[32,32,256]{2,1,0:T(8,128)(2,1)S(1)} %all_to_all.30.got_ref.triangle_ref, ...), custom_call_target="tpu_custom_call" | custom-call | flops 402653184 | bytes 9110528 | tf_op jit(solution)/shard_map/pallas_call | solution.py:44
  146.3 2.6 %all-to-all-done.5.full_ref = bf16[32,24,128]{2,1,0:T(8,128)(2,1)S(1)} async-done(((bf16[32,24,128]{2,1,0:T(8,128)(2,1)}), bf16[32,24,128]{2,1,0:T(8,128)(2,1)S(1)}, u32[]{:S(2)}, u32[]{:S(2)}) %all-to-all-start.5) | async-done | bytes 196640 | tf_op jit(solution)/shard_map/all_to_all | solution.py:29
  148.9 0.8 shard_map.116
  (1 shorter events, 0.0 us)
Async XLA Ops:
  3.8 36.3 %all-to-all-start = ((bf16[32,64,256]{2,1,0:T(8,128)(2,1)}), bf16[32,64,256]{2,1,0:T(8,128)(2,1)S(1)}, u32[]{:S(2)}, u32[]{:S(2)}) async-start(bf16[32,64,256]{2,1,0:T(8,128)(2,1)} %shard_map.109), calls=%async_computation | async-start | bytes 2097152 | tf_op jit(solution)/shard_map/all_to_all | solution.py:29
  15.0 1.0 copy-start.3
  16.1 1.0 copy-start.5
  17.1 0.9 copy-start.7
  18.0 0.8 copy-start.13
  18.8 0.7 copy-start.15
  19.4 0.7 copy-start.17
  23.3 2.4 %copy-start = (f32[8,640,256]{2,1,0:T(8,128)}, f32[8,640,256]{2,1,0:T(8,128)S(1)}, u32[]{:S(2)}) copy-start(f32[8,640,256]{2,1,0:T(8,128)S(1)} %get-tuple-element.47.factor_ref) | copy-start | bytes 15728644
  25.7 0.8 copy-start.9
  26.5 14.0 %copy-start.11 = (bf16[8,128,256]{2,1,0:T(8,128)(2,1)}, bf16[8,128,256]{2,1,0:T(8,128)(2,1)S(1)}, u32[]{:S(2)}) copy-start(bf16[8,128,256]{2,1,0:T(8,128)(2,1)S(1)} %get-tuple-element.45.grad_out_ref) | copy-start | bytes 1572868
  26.5 89.4 %copy-start.4 = (bf16[8,256,128]{2,1,0:T(8,128)(2,1)S(1)}, bf16[8,256,128]{2,1,0:T(8,128)(2,1)}, u32[]{:S(2)}) copy-start(bf16[8,256,128]{2,1,0:T(8,128)(2,1)} %cot_ref.2) | copy-start | bytes 1572868
  26.5 89.4 %copy-start.14 = (bf16[128,128]{1,0:T(8,128)(2,1)S(1)}, bf16[128,128]{1,0:T(8,128)(2,1)}, u32[]{:S(2)}) copy-start(bf16[128,128]{1,0:T(8,128)(2,1)} %w_out_ref.7) | copy-start | bytes 98308
  26.5 89.4 %copy-start.18 = (f32[128]{0:T(128)S(1)}, f32[128]{0:T(128)}, u32[]{:S(2)}) copy-start(f32[128]{0:T(128)} %param.9) | copy-start | bytes 1540
  40.1 75.8 %copy-start.1 = (f32[8,640,256]{2,1,0:T(8,128)S(1)}, f32[8,640,256]{2,1,0:T(8,128)}, u32[]{:S(2)}) copy-start(f32[8,640,256]{2,1,0:T(8,128)} %copy-done) | copy-start | bytes 15728644
  40.1 75.8 %copy-start.10 = (bf16[8,128,256]{2,1,0:T(8,128)(2,1)S(1)}, bf16[8,128,256]{2,1,0:T(8,128)(2,1)}, u32[]{:S(2)}) copy-start(bf16[8,128,256]{2,1,0:T(8,128)(2,1)} %copy-done.9) | copy-start | bytes 1572868
  40.5 75.5 %copy-start.12 = (bf16[8,128,256]{2,1,0:T(8,128)(2,1)S(1)}, bf16[8,128,256]{2,1,0:T(8,128)(2,1)}, u32[]{:S(2)}) copy-start(bf16[8,128,256]{2,1,0:T(8,128)(2,1)} %copy-done.11) | copy-start | bytes 1572868
  116.0 24.1 %copy-start.6 = (bf16[8,256,128]{2,1,0:T(8,128)(2,1)S(1)}, bf16[8,256,128]{2,1,0:T(8,128)(2,1)}, u32[]{:S(2)}) copy-start(bf16[8,256,128]{2,1,0:T(8,128)(2,1)} %pair_ref.1) | copy-start | bytes 1572868
  116.0 24.1 %copy-start.8 = (bf16[128,640]{1,0:T(8,128)(2,1)S(1)}, bf16[128,640]{1,0:T(8,128)(2,1)}, u32[]{:S(2)}) copy-start(bf16[128,640]{1,0:T(8,128)(2,1)} %weight_ref.5) | copy-start | bytes 491524
  116.0 24.1 %copy-start.16 = (f32[128]{0:T(128)S(1)}, f32[128]{0:T(128)}, u32[]{:S(2)}) copy-start(f32[128]{0:T(128)} %param.7) | copy-start | bytes 1540
  134.7 14.1 %all-to-all-start.5 = ((bf16[32,24,128]{2,1,0:T(8,128)(2,1)}), bf16[32,24,128]{2,1,0:T(8,128)(2,1)S(1)}, u32[]{:S(2)}, u32[]{:S(2)}) async-start(bf16[32,24,128]{2,1,0:T(8,128)(2,1)} %broadcast_in_dim.8), calls=%async_computation.5 | async-start | bytes 393216 | tf_op jit(solution)/shard_map/all_to_all | solution.py:29
  140.1 2.5 %copy-start.2 = (f32[8,640,256]{2,1,0:T(8,128)S(1)}, f32[8,640,256]{2,1,0:T(8,128)}, u32[]{:S(2)}) copy-start(f32[8,640,256]{2,1,0:T(8,128)} %copy-done) | copy-start | bytes 15728644

commit v6 on v5

--- a/solution.py
+++ b/solution.py
@@ -29,11 +29,24 @@
     return lax.all_to_all(values, "dap", 0, 0, tiled=True, axis_index_groups=groups)
 
 
+def exchange_chips(values):
+    chips = range(values.shape[0])
+    if values.shape[0] % 8 == 0:
+        chips = [high + z for high in chips[::8] for z in (0, 3, 4, 7, 1, 2, 5, 6)]
+    groups = [[2 * chip + core for chip in chips] for core in range(2)]
+    return lax.all_to_all(values, "dap", 0, 0, tiled=True, axis_index_groups=groups)
+
+
+def swap(values):
+    devices = lax.axis_size("dap")
+    return lax.ppermute(values, "dap", [(d, d ^ 1) for d in range(devices)])
+
+
 def hold(*values):
     return lax.optimization_barrier(values)
 
 
-def call(kernel, out_shape, operands, scratch=(), flops=0, outside=0, limit=16, leave=False):
+def call(kernel, out_shape, operands, scratch=(), flops=0, outside=0, limit=16, scalars=0, leave=False):
     leaves = out_shape if isinstance(out_shape, (tuple, list)) else [out_shape]
     moved = sum(a.size * a.dtype.itemsize for a in list(operands) + list(leaves))
     spec = pl.BlockSpec(memory_space=pltpu.VMEM)
@@ -44,7 +57,9 @@
     return pl.pallas_call(
         kernel,
         out_shape=out_shape,
-        in_specs=[pl.BlockSpec(memory_space=pltpu.HBM)] * outside + [spec] * (len(operands) - outside),
+        in_specs=[pl.BlockSpec(memory_space=pltpu.HBM)] * outside
+        + [pl.BlockSpec(memory_space=pltpu.SMEM)] * scalars
+        + [spec] * (len(operands) - outside - scalars),
         out_specs=out_specs,
         scratch_shapes=list(scratch),
         cost_estimate=pl.CostEstimate(flops=flops, bytes_accessed=moved, transcendentals=0),
@@ -271,6 +286,7 @@
 
 
 def weight_grads_kernel(
+    core_ref,
     got_ref,
     factor_ref,
     normed_ref,
@@ -279,10 +295,12 @@
     grad_out_ref,
     gain_out_ref,
     w_out_ref,
-    sent_ref,
+    keep_ref,
+    send_ref,
     left_ref,
     right_ref,
     turned_ref,
+    halves_ref,
 ):
     rows = normed_ref.shape[0]
     fill(got_ref, left_ref, right_ref)
@@ -298,7 +316,16 @@
         pairs = [(normed_ref[i], grad) for grad in grads] + [(out_normed, grad_out_ref[i])]
         parts = [lax.dot_general(x, y, NT, preferred_element_type=F32) for x, y in pairs]
         total = parts if total is None else [x + y for x, y in zip(total, parts)]
-    sent_ref[...] = jnp.concatenate(total, axis=0).reshape(sent_ref.shape).astype(BF16)
+    halves_ref[0] = jnp.concatenate(total[:3], axis=0)
+    halves_ref[1] = jnp.concatenate(total[3:], axis=0)
+    core = core_ref[0]
+    keep_ref[...] = halves_ref[core]
+    send_ref[...] = halves_ref[1 - core].astype(BF16)
+
+
+def add_kernel(keep_ref, other_ref, sent_ref):
+    total = keep_ref[...] + other_ref[...].astype(F32)
+    sent_ref[...] = total.astype(BF16).reshape(sent_ref.shape)
 
 
 def pair_grad_kernel(
@@ -338,10 +365,24 @@
         out_ref[i] = grad_pair.T.astype(BF16)
 
 
-def finish_kernel(full_ref, weight_ref, w_out_ref, gain_in_ref, gain_out_ref, *outs):
-    grad_weight_ref, grad_out_ref, grad_gain_in_ref, grad_gain_out_ref = outs
+def sum_kernel(got_ref, sent_ref):
+    total = got_ref[0].astype(F32)
+    for m in range(1, got_ref.shape[0]):
+        total = total + got_ref[m].astype(F32)
+    total = total.astype(BF16)
+    for m in range(sent_ref.shape[0]):
+        sent_ref[m] = total
+
+
+def finish_kernel(
+    core_ref, own_ref, other_ref, weight_ref, w_out_ref, gain_in_ref, gain_out_ref, *outs
+):
+    grad_weight_ref, grad_out_ref, grad_gain_in_ref, grad_gain_out_ref, halves_ref = outs
     width = w_out_ref.shape[0]
-    full = full_ref[...].astype(F32).reshape(6 * width, width)
+    core = core_ref[0]
+    halves_ref[core] = own_ref[...].astype(F32).reshape(3 * width, width)
+    halves_ref[1 - core] = other_ref[...].astype(F32).reshape(3 * width, width)
+    full = halves_ref[...].reshape(6 * width, width)
     weight = weight_ref[...].astype(F32)
     total = jnp.zeros((width, width), F32)
     for b in range(5):
@@ -375,7 +416,8 @@
         leave=True,
         limit=62,
     )
-    sent, pair, cotangent = hold(sent, pair, cotangent)
+    core = lax.rem(lax.axis_index("dap"), 2).astype(jnp.int32)[None]
+    sent, pair, cotangent, core = hold(sent, pair, cotangent, core)
     got = exchange(sent)
 
     turned = shape((rows, width, res), BF16)
@@ -390,7 +432,9 @@
         (pair, cotangent, gain_in[None], gain_out[None], w_proj, w_out),
         flops=2 * rows * res * width * 6 * width,
     )
-    got, normed, factor, grad_proj_out, scaled = hold(got, normed, factor, grad_proj_out, scaled)
+    got, normed, factor, grad_proj_out, scaled, core = hold(
+        got, normed, factor, grad_proj_out, scaled, core
+    )
     edge = shape((share, devices * rows, res), BF16)
     sent, left, right = call(
         functools.partial(triangle_kernel, share, rows),
@@ -410,17 +454,20 @@
         (got, left, right),
     )
     got = exchange(sent)
-    sent = call(
+    chips = devices // 2
+    half_shape = (3 * width, width)
+    keep, send = call(
         weight_grads_kernel,
-        shape((devices, 6 * width // devices, width), BF16),
-        (got, factor, normed, triangle, cotangent, grad_proj_out, gain_out[None], w_out),
-        scratch + scratch[:1],
-    )
-    sums = exchange(sent)
-    mine = jnp.sum(sums.astype(F32), axis=0).astype(BF16)
-    mine = jnp.broadcast_to(mine[None], (devices,) + mine.shape)
+        (shape(half_shape, F32), shape(half_shape, BF16)),
+        (core, got, factor, normed, triangle, cotangent, grad_proj_out, gain_out[None], w_out),
+        scratch + scratch[:1] + [pltpu.VMEM((2,) + half_shape, F32)],
+        scalars=1,
+    )
+    sent = call(add_kernel, shape((chips, 3 * width // chips, width), BF16), (keep, swap(send)))
+    sums = exchange_chips(sent)
+    mine = call(sum_kernel, shape(sums.shape, BF16), (sums,))
     mine, edge_grads, factor, triangle = hold(mine, got, factor, triangle)
-    full = exchange(mine)
+    own = exchange_chips(mine)
     grad_pair, update = call(
         pair_grad_kernel,
         [shape((rows, res, width), BF16)] * 2,
@@ -429,6 +476,7 @@
         scratch + scratch[:1],
         flops=2 * rows * res * width * 6 * width,
     )
+    own, grad_pair, update = hold(own, grad_pair, update)
     grad_w_proj, grad_w_out, grad_gain_in, grad_gain_out = call(
         finish_kernel,
         (
@@ -437,7 +485,9 @@
             shape((1, width), F32),
             shape((1, width), F32),
         ),
-        (full, w_proj, w_out, gain_in[None], gain_out[None]),
+        (core, own, swap(own), w_proj, w_out, gain_in[None], gain_out[None]),
+        [pltpu.VMEM((2,) + half_shape, F32)],
+        scalars=1,
     )
     return (update, grad_pair, grad_gain_in[0], grad_w_proj, grad_gain_out[0], grad_w_out)
 

time: 150 us -> 151 us (level)
  blocking collectives: 90.2 us -> 86.2 us
  starting transfers between devices: 16.5 us -> 20.3 us
    all_to_all x4 -> x3, blocking collectives: 90.2 us -> 74.5 us  [exchange(): lax.all_to_all(values, 'dap', 0, 0, tiled=True, axis_index_groups=groups)]
    all_to_all x0 -> x1, blocking collectives: none -> 11.7 us  [exchange_chips(): lax.all_to_all(values, 'dap', 0, 0, tiled=True, axis_index_groups=groups)]
    ppermute x0 -> x2, starting transfers between devices: none -> 5.63 us  [swap(): return lax.ppermute(values, 'dap', [(d, d ^ 1) for d in range(devices)])]
    all_to_all x2 -> x1, starting transfers between devices: 16.5 us -> 11.2 us  [exchange(): lax.all_to_all(values, 'dap', 0, 0, tiled=True, axis_index_groups=groups)]
    all_to_all x0 -> x1, starting transfers between devices: none -> 3.51 us  [exchange_chips(): lax.all_to_all(values, 'dap', 0, 0, tiled=True, axis_index_groups=groups)]
    all_to_all x2 -> x1, waiting for transfers between devices: 16.2 us -> 13.6 us  [exchange(): lax.all_to_all(values, 'dap', 0, 0, tiled=True, axis_index_groups=groups)]
    ppermute x0 -> x2, waiting for transfers between devices: none -> 1.89 us  [swap(): return lax.ppermute(values, 'dap', [(d, d ^ 1) for d in range(devices)])]
    pallas_call x8 -> x10, Pallas kernels: 14.4 us -> 14.9 us  [call(): pl.pallas_call(kernel, out_shape=out_shape, in_specs=[pl.BlockSpec(memory...]
  transfers between devices with their start and end apart: 2 -> 4, of which waited for: 2 -> 4; matrix products, arithmetic and copies ran while one was open for 0% -> 0% of each run, Pallas kernels for 5% -> 5%
where the time goes in v6:
time: 151 us; the launch traced here: 150 us
  blocking collectives  86.2 us (57%)
  starting transfers between devices  20.3 us (13%)
  waiting for transfers between devices  17 us (11%)
  Pallas kernels  14.9 us (10%)
  local copies, waits for them, and re-layouts  10.7 us (7%)
    all_to_all x3, blocking collectives, exchange(): lax.all_to_all(values, 'dap', 0, 0, tiled=True, axis_index_groups=groups)  74.5 us
    pallas_call x10, Pallas kernels, call(): pl.pallas_call(kernel, out_shape=out_shape, in_specs=[pl.BlockSpec(memory...  14.9 us
    all_to_all x1, waiting for transfers between devices, exchange(): lax.all_to_all(values, 'dap', 0, 0, tiled=True, axis_index_groups=groups)  13.6 us
    all_to_all x1, blocking collectives, exchange_chips(): lax.all_to_all(values, 'dap', 0, 0, tiled=True, axis_index_groups=groups)  11.7 us
    all_to_all x1, starting transfers between devices, exchange(): lax.all_to_all(values, 'dap', 0, 0, tiled=True, axis_index_groups=groups)  11.2 us
    unnamed x38, local copies, waits for them, and re-layouts  10.7 us
    ppermute x2, starting transfers between devices, swap(): return lax.ppermute(values, 'dap', [(d, d ^ 1) for d in range(devices)])  5.63 us
    all_to_all x1, starting transfers between devices, exchange_chips(): lax.all_to_all(values, 'dap', 0, 0, tiled=True, axis_index_groups=groups)  3.51 us
  transfers between devices with their start and end apart: 4, of which 4 were waited for; matrix products, arithmetic and copies ran while one was open for 0% of the time, Pallas kernels for 5%

profile of v6, /device:TPU:1, one launch (start us, length us, event | category | flops | bytes accessed | tf_op | source)
XLA Modules:
  0.0 149.9 jit_solution(12837322978670018680)
XLA Ops:
  0.6 3.2 %shard_map.109 = bf16[32,64,256]{2,1,0:T(8,128)(2,1)} custom-call(bf16[8,256,128]{2,1,0:T(8,128)(2,1)} %pair_ref.1, f32[1,128]{1,0:T(1,128)} %bitcast.5, bf16[128,640]{1,0:T(8,128)(2,1)} %weight_ref.5), custom_call_target="tpu_custom_call" | custom-call | bytes 1737216 | tf_op jit(solution)/shard_map/pallas_call | solution.py:57
  3.8 11.2 %all-to-all-start = ((bf16[32,64,256]{2,1,0:T(8,128)(2,1)}), bf16[32,64,256]{2,1,0:T(8,128)(2,1)S(1)}, u32[]{:S(2)}, u32[]{:S(2)}) async-start(bf16[32,64,256]{2,1,0:T(8,128)(2,1)} %shard_map.109), calls=%async_computation | async-start | bytes 2097152 | tf_op jit(solution)/shard_map/all_to_all | solution.py:29
  15.0 0.0 copy-start.3
  15.0 1.0 copy-done.3
  16.0 0.0 copy-start.5
  16.1 1.0 copy-done.5
  17.1 0.0 copy-start.7
  17.1 0.9 copy-done.7
  18.0 0.0 copy-start.13
  18.0 0.8 copy-done.13
  18.8 0.0 copy-start.15
  18.8 0.7 copy-done.15
  19.4 0.0 copy-start.17
  19.4 0.7 copy-done.17
  20.1 3.2 %shard_map.110 = (bf16[8,128,256]{2,1,0:T(8,128)(2,1)S(1)}, f32[8,640,256]{2,1,0:T(8,128)S(1)}, bf16[8,128,256]{2,1,0:T(8,128)(2,1)S(1)}, f32[2,1024,128]{2,1,0:T(8,128)S(1)}) custom-call(bf16[8,256,128]{2,1,0:T(8,128)(2,1)S(1)} %copy-done.5, bf16[8,256,128]{2,1,0:T(8,128)(2,1)S(1)} %copy-done.3, f32[1,128]{1,0:T(1,128)S(1)} %bitcast.6, ...), custom_call_target="tpu_custom_call" | custom-call | flops 402653184 | bytes 8586240 | tf_op jit(solution)/shard_map/pallas_call | solution.py:57
  23.3 0.0 copy-start
  23.3 2.3 %copy-done = f32[8,640,256]{2,1,0:T(8,128)} copy-done((f32[8,640,256]{2,1,0:T(8,128)}, f32[8,640,256]{2,1,0:T(8,128)S(1)}, u32[]{:S(2)}) %copy-start) | copy-done | bytes 5242904
  25.7 0.0 copy-start.9
  25.7 0.8 copy-done.9
  26.5 0.0 copy-start.11
  26.5 0.0 copy-start.4
  26.5 0.0 copy-start.14
  26.5 0.0 copy-start.18
  26.5 13.6 %all-to-all-done.got_ref = bf16[32,64,256]{2,1,0:T(8,128)(2,1)S(1)} async-done(((bf16[32,64,256]{2,1,0:T(8,128)(2,1)}), bf16[32,64,256]{2,1,0:T(8,128)(2,1)S(1)}, u32[]{:S(2)}, u32[]{:S(2)}) %all-to-all-start) | async-done | bytes 1048608 | tf_op jit(solution)/shard_map/all_to_all | solution.py:29
  40.1 0.0 copy-start.1
  40.1 0.0 copy-start.10
  40.1 0.4 shard_map.111
  40.5 0.0 copy-done.11
  40.5 0.0 copy-start.12
  40.5 21.3 %all_to_all.30.got_ref.triangle_ref = bf16[32,32,256]{2,1,0:T(8,128)(2,1)S(1)} all-to-all(bf16[32,32,256]{2,1,0:T(8,128)(2,1)S(1)} %get-tuple-element.48), channel_id=1, replica_groups={{0,6,8,14,2,4,10,12,1,7,9,15,3,5,11,13,17,23,25,31,19,21,27,29,16,22,24..., dimensions={0} | all-to-all | bytes 1048576 | tf_op jit(solution)/shard_map/all_to_all | solution.py:29
  61.8 0.6 shard_map.112
  62.4 21.0 %all_to_all.31.got_ref = bf16[32,32,256]{2,1,0:T(8,128)(2,1)S(1)} all-to-all(bf16[32,32,256]{2,1,0:T(8,128)(2,1)S(1)} %shard_map.112), channel_id=1, replica_groups={{0,6,8,14,2,4,10,12,1,7,9,15,3,5,11,13,17,23,25,31,19,21,27,29,16,22,24..., dimensions={0} | all-to-all | bytes 1048576 | tf_op jit(solution)/shard_map/all_to_all | solution.py:29
  83.3 0.5 shard_map.113
  83.8 0.0 copy-start.6
  83.8 0.0 copy-start.8
  83.8 0.0 copy-start.16
  83.9 32.2 %all_to_all.32.got_ref = bf16[32,64,256]{2,1,0:T(8,128)(2,1)S(1)} all-to-all(bf16[32,64,256]{2,1,0:T(8,128)(2,1)S(1)} %shard_map.113), channel_id=1, replica_groups={{0,6,8,14,2,4,10,12,1,7,9,15,3,5,11,13,17,23,25,31,19,21,27,29,16,22,24..., dimensions={0} | all-to-all | bytes 2097152 | tf_op jit(solution)/shard_map/all_to_all | solution.py:29
  116.1 0.0 copy-done.4
  116.1 0.0 copy-done.14
  116.1 0.0 copy-done.18
  116.1 0.0 copy-done.1
  116.1 0.0 copy-done.10
  116.1 0.0 copy-done.12
  116.1 2.0 %shard_map.114 = (f32[384,128]{1,0:T(8,128)S(1)}, bf16[384,128]{1,0:T(8,128)(2,1)S(1)}) custom-call(s32[1]{0:T(128)} %bitcast.1.core_ref, bf16[32,64,256]{2,1,0:T(8,128)(2,1)S(1)} %all_to_all.32.got_ref, f32[8,640,256]{2,1,0:T(8,128)S(1)} %copy-done.1, bf16[8,128,256]{2,1,0:T(8,128)(2,1)S(1)} %copy-done.10, ...), custom_call_target="tpu_custom_call" | custom-call | bytes 8716804 | tf_op jit(solution)/shard_map/pallas_call | solution.py:57
  118.1 2.7 %collective-permute-start = (bf16[384,128]{1,0:T(8,128)(2,1)S(1)}, bf16[384,128]{1,0:T(8,128)(2,1)S(1)}, u32[]{:S(2)}, u32[]{:S(2)}) collective-permute-start(bf16[384,128]{1,0:T(8,128)(2,1)S(1)} %get-tuple-element.56), channel_id=1, source_target_pairs={{0,1},{1,0},{2,3},{3,2},{4,5},{5,4},{6,7},{7,6},{8,9},{9,8},{10,11... | collective-permute-start | bytes 294920 | tf_op jit(solution)/shard_map/ppermute | solution.py:42
  120.9 0.9 collective-permute-done.other_ref
  121.8 11.7 %all_to_all.33.got_ref = bf16[16,24,128]{2,1,0:T(8,128)(2,1)S(1)} all-to-all(bf16[16,24,128]{2,1,0:T(8,128)(2,1)S(1)} %shard_map.115), channel_id=1, replica_groups={{0,6,8,14,2,4,10,12,16,22,24,30,18,20,26,28},{1,7,9,15,3,5,11,13,17,23,..., dimensions={0} | all-to-all | bytes 196608 | tf_op jit(solution)/shard_map/all_to_all | solution.py:37
  133.5 0.7 shard_map.116
  134.2 3.5 %all-to-all-start.5 = ((bf16[16,24,128]{2,1,0:T(8,128)(2,1)}), bf16[16,24,128]{2,1,0:T(8,128)(2,1)S(1)}, u32[]{:S(2)}, u32[]{:S(2)}) async-start(bf16[16,24,128]{2,1,0:T(8,128)(2,1)} %shard_map.116), calls=%async_computation.5 | async-start | bytes 196608 | tf_op jit(solution)/shard_map/all_to_all | solution.py:37
  137.7 0.0 copy-done.6
  137.7 0.0 copy-done.8
  137.7 0.0 copy-done.16
  137.7 0.0 copy-start.2
  137.7 2.5 %copy-done.2 = f32[8,640,256]{2,1,0:T(8,128)S(1)} copy-done((f32[8,640,256]{2,1,0:T(8,128)S(1)}, f32[8,640,256]{2,1,0:T(8,128)}, u32[]{:S(2)}) %copy-start.2) | copy-done | bytes 5242904
  140.2 3.5 %shard_map.117 = (bf16[8,256,128]{2,1,0:T(8,128)(2,1)}, bf16[8,256,128]{2,1,0:T(8,128)(2,1)}) custom-call(bf16[32,64,256]{2,1,0:T(8,128)(2,1)S(1)} %all_to_all.32.got_ref, f32[8,640,256]{2,1,0:T(8,128)S(1)} %copy-done.2, bf16[8,256,128]{2,1,0:T(8,128)(2,1)S(1)} %copy-done.6, bf16[32,32,256]{2,1,0:T(8,128)(2,1)S(1)} %all_to_all.30.got_ref.triangle_ref, ...), custom_call_target="tpu_custom_call" | custom-call | flops 402653184 | bytes 9110528 | tf_op jit(solution)/shard_map/pallas_call | solution.py:57
  143.8 1.5 all-to-all-done.5.own_ref
  145.2 2.9 %collective-permute-start.1 = (bf16[16,24,128]{2,1,0:T(8,128)(2,1)S(1)}, bf16[16,24,128]{2,1,0:T(8,128)(2,1)S(1)}, u32[]{:S(2)}, u32[]{:S(2)}) collective-permute-start(bf16[16,24,128]{2,1,0:T(8,128)(2,1)S(1)} %all-to-all-done.5.own_ref), channel_id=1, source_target_pairs={{0,1},{1,0},{2,3},{3,2},{4,5},{5,4},{6,7},{7,6},{8,9},{9,8},{10,11... | collective-permute-start | bytes 294920 | tf_op jit(solution)/shard_map/ppermute | solution.py:42
  148.1 0.9 collective-permute-done.1.other_ref
  149.1 0.8 shard_map.118
  (1 shorter events, 0.0 us)
Async XLA Ops:
  3.8 36.3 %all-to-all-start = ((bf16[32,64,256]{2,1,0:T(8,128)(2,1)}), bf16[32,64,256]{2,1,0:T(8,128)(2,1)S(1)}, u32[]{:S(2)}, u32[]{:S(2)}) async-start(bf16[32,64,256]{2,1,0:T(8,128)(2,1)} %shard_map.109), calls=%async_computation | async-start | bytes 2097152 | tf_op jit(solution)/shard_map/all_to_all | solution.py:29
  15.0 1.0 copy-start.3
  16.0 1.0 copy-start.5
  17.1 0.9 copy-start.7
  18.0 0.8 copy-start.13
  18.8 0.7 copy-start.15
  19.4 0.7 copy-start.17
  23.3 2.3 %copy-start = (f32[8,640,256]{2,1,0:T(8,128)}, f32[8,640,256]{2,1,0:T(8,128)S(1)}, u32[]{:S(2)}) copy-start(f32[8,640,256]{2,1,0:T(8,128)S(1)} %get-tuple-element.59.factor_ref) | copy-start | bytes 15728644
  25.7 0.8 copy-start.9
  26.5 14.0 %copy-start.11 = (bf16[8,128,256]{2,1,0:T(8,128)(2,1)}, bf16[8,128,256]{2,1,0:T(8,128)(2,1)S(1)}, u32[]{:S(2)}) copy-start(bf16[8,128,256]{2,1,0:T(8,128)(2,1)S(1)} %get-tuple-element.54.grad_out_ref) | copy-start | bytes 1572868
  26.5 89.6 %copy-start.4 = (bf16[8,256,128]{2,1,0:T(8,128)(2,1)S(1)}, bf16[8,256,128]{2,1,0:T(8,128)(2,1)}, u32[]{:S(2)}) copy-start(bf16[8,256,128]{2,1,0:T(8,128)(2,1)} %cot_ref.2) | copy-start | bytes 1572868
  26.5 89.6 %copy-start.14 = (bf16[128,128]{1,0:T(8,128)(2,1)S(1)}, bf16[128,128]{1,0:T(8,128)(2,1)}, u32[]{:S(2)}) copy-start(bf16[128,128]{1,0:T(8,128)(2,1)} %w_out_ref.7) | copy-start | bytes 98308
  26.5 89.6 %copy-start.18 = (f32[128]{0:T(128)S(1)}, f32[128]{0:T(128)}, u32[]{:S(2)}) copy-start(f32[128]{0:T(128)} %param.9) | copy-start | bytes 1540
  40.1 76.0 %copy-start.1 = (f32[8,640,256]{2,1,0:T(8,128)S(1)}, f32[8,640,256]{2,1,0:T(8,128)}, u32[]{:S(2)}) copy-start(f32[8,640,256]{2,1,0:T(8,128)} %copy-done) | copy-start | bytes 15728644
  40.1 76.0 %copy-start.10 = (bf16[8,128,256]{2,1,0:T(8,128)(2,1)S(1)}, bf16[8,128,256]{2,1,0:T(8,128)(2,1)}, u32[]{:S(2)}) copy-start(bf16[8,128,256]{2,1,0:T(8,128)(2,1)} %copy-done.9) | copy-start | bytes 1572868
  40.5 75.6 %copy-start.12 = (bf16[8,128,256]{2,1,0:T(8,128)(2,1)S(1)}, bf16[8,128,256]{2,1,0:T(8,128)(2,1)}, u32[]{:S(2)}) copy-start(bf16[8,128,256]{2,1,0:T(8,128)(2,1)} %copy-done.11) | copy-start | bytes 1572868
  83.8 53.9 %copy-start.6 = (bf16[8,256,128]{2,1,0:T(8,128)(2,1)S(1)}, bf16[8,256,128]{2,1,0:T(8,128)(2,1)}, u32[]{:S(2)}) copy-start(bf16[8,256,128]{2,1,0:T(8,128)(2,1)} %pair_ref.1) | copy-start | bytes 1572868
  83.8 53.9 %copy-start.8 = (bf16[128,640]{1,0:T(8,128)(2,1)S(1)}, bf16[128,640]{1,0:T(8,128)(2,1)}, u32[]{:S(2)}) copy-start(bf16[128,640]{1,0:T(8,128)(2,1)} %weight_ref.5) | copy-start | bytes 491524
  83.8 53.9 %copy-start.16 = (f32[128]{0:T(128)S(1)}, f32[128]{0:T(128)}, u32[]{:S(2)}) copy-start(f32[128]{0:T(128)} %param.7) | copy-start | bytes 1540
  118.1 3.7 %collective-permute-start = (bf16[384,128]{1,0:T(8,128)(2,1)S(1)}, bf16[384,128]{1,0:T(8,128)(2,1)S(1)}, u32[]{:S(2)}, u32[]{:S(2)}) collective-permute-start(bf16[384,128]{1,0:T(8,128)(2,1)S(1)} %get-tuple-element.56), channel_id=1, source_target_pairs={{0,1},{1,0},{2,3},{3,2},{4,5},{5,4},{6,7},{7,6},{8,9},{9,8},{10,11... | collective-permute-start | bytes 294920 | tf_op jit(solution)/shard_map/ppermute | solution.py:42
  134.2 11.0 %all-to-all-start.5 = ((bf16[16,24,128]{2,1,0:T(8,128)(2,1)}), bf16[16,24,128]{2,1,0:T(8,128)(2,1)S(1)}, u32[]{:S(2)}, u32[]{:S(2)}) async-start(bf16[16,24,128]{2,1,0:T(8,128)(2,1)} %shard_map.116), calls=%async_computation.5 | async-start | bytes 196608 | tf_op jit(solution)/shard_map/all_to_all | solution.py:37
  137.7 2.5 %copy-start.2 = (f32[8,640,256]{2,1,0:T(8,128)S(1)}, f32[8,640,256]{2,1,0:T(8,128)}, u32[]{:S(2)}) copy-start(f32[8,640,256]{2,1,0:T(8,128)} %copy-done) | copy-start | bytes 15728644
  145.2 3.8 %collective-permute-start.1 = (bf16[16,24,128]{2,1,0:T(8,128)(2,1)S(1)}, bf16[16,24,128]{2,1,0:T(8,128)(2,1)S(1)}, u32[]{:S(2)}, u32[]{:S(2)}) collective-permute-start(bf16[16,24,128]{2,1,0:T(8,128)(2,1)S(1)} %all-to-all-done.5.own_ref), channel_id=1, source_target_pairs={{0,1},{1,0},{2,3},{3,2},{4,5},{5,4},{6,7},{7,6},{8,9},{9,8},{10,11... | collective-permute-start | bytes 294920 | tf_op jit(solution)/shard_map/ppermute | solution.py:42

commit v7 on v6

--- a/solution.py
+++ b/solution.py
@@ -29,10 +29,15 @@
     return lax.all_to_all(values, "dap", 0, 0, tiled=True, axis_index_groups=groups)
 
 
+def chips_of(members):
+    chips = range(members)
+    if members % 8 == 0:
+        chips = [high + z for high in chips[::8] for z in (0, 3, 4, 7, 1, 2, 5, 6)]
+    return list(chips)
+
+
 def exchange_chips(values):
-    chips = range(values.shape[0])
-    if values.shape[0] % 8 == 0:
-        chips = [high + z for high in chips[::8] for z in (0, 3, 4, 7, 1, 2, 5, 6)]
+    chips = chips_of(values.shape[0])
     groups = [[2 * chip + core for chip in chips] for core in range(2)]
     return lax.all_to_all(values, "dap", 0, 0, tiled=True, axis_index_groups=groups)
 
@@ -375,14 +380,14 @@
 
 
 def finish_kernel(
-    core_ref, own_ref, other_ref, weight_ref, w_out_ref, gain_in_ref, gain_out_ref, *outs
+    full_ref, weight_ref, w_out_ref, gain_in_ref, gain_out_ref, *outs
 ):
-    grad_weight_ref, grad_out_ref, grad_gain_in_ref, grad_gain_out_ref, halves_ref = outs
+    grad_weight_ref, grad_out_ref, grad_gain_in_ref, grad_gain_out_ref = outs
     width = w_out_ref.shape[0]
-    core = core_ref[0]
-    halves_ref[core] = own_ref[...].astype(F32).reshape(3 * width, width)
-    halves_ref[1 - core] = other_ref[...].astype(F32).reshape(3 * width, width)
-    full = halves_ref[...].reshape(6 * width, width)
+    devices = full_ref.shape[0]
+    order = places(devices)
+    slots = [order.index(2 * c + core) for core in range(2) for c in chips_of(devices // 2)]
+    full = jnp.concatenate([full_ref[m].astype(F32) for m in slots], axis=0)
     weight = weight_ref[...].astype(F32)
     total = jnp.zeros((width, width), F32)
     for b in range(5):
@@ -465,9 +470,9 @@
     )
     sent = call(add_kernel, shape((chips, 3 * width // chips, width), BF16), (keep, swap(send)))
     sums = exchange_chips(sent)
-    mine = call(sum_kernel, shape(sums.shape, BF16), (sums,))
+    mine = call(sum_kernel, shape((devices,) + sums.shape[1:], BF16), (sums,))
     mine, edge_grads, factor, triangle = hold(mine, got, factor, triangle)
-    own = exchange_chips(mine)
+    own = exchange(mine)
     grad_pair, update = call(
         pair_grad_kernel,
         [shape((rows, res, width), BF16)] * 2,
@@ -485,9 +490,7 @@
             shape((1, width), F32),
             shape((1, width), F32),
         ),
-        (core, own, swap(own), w_proj, w_out, gain_in[None], gain_out[None]),
-        [pltpu.VMEM((2,) + half_shape, F32)],
-        scalars=1,
+        (own, w_proj, w_out, gain_in[None], gain_out[None]),
     )
     return (update, grad_pair, grad_gain_in[0], grad_w_proj, grad_gain_out[0], grad_w_out)
 

time: 151 us -> 150 us (level)
    all_to_all x1 -> x2, starting transfers between devices: 11.2 us -> 16.4 us  [exchange(): lax.all_to_all(values, 'dap', 0, 0, tiled=True, axis_index_groups=groups)]
    all_to_all x1 -> x0, starting transfers between devices: 3.51 us -> none  [exchange_chips(): lax.all_to_all(values, 'dap', 0, 0, tiled=True, axis_index_groups=groups)]
    ppermute x2 -> x1, starting transfers between devices: 5.63 us -> 2.73 us  [swap(): return lax.ppermute(values, 'dap', [(d, d ^ 1) for d in range(devices)])]
    all_to_all x1 -> x2, waiting for transfers between devices: 13.6 us -> 16.5 us  [exchange(): lax.all_to_all(values, 'dap', 0, 0, tiled=True, axis_index_groups=groups)]
  transfers between devices with their start and end apart: 4 -> 3, of which waited for: 4 -> 3; matrix products, arithmetic and copies ran while one was open for 0% -> 0% of each run, Pallas kernels for 5% -> 5%
where the time goes in v7:
time: 150 us; the launch traced here: 149 us
  blocking collectives  86 us (57%)
  starting transfers between devices  19.1 us (13%)
  waiting for transfers between devices  17.4 us (12%)
  Pallas kernels  15.2 us (10%)
  local copies, waits for them, and re-layouts  10.7 us (7%)
    all_to_all x3, blocking collectives, exchange(): lax.all_to_all(values, 'dap', 0, 0, tiled=True, axis_index_groups=groups)  74.4 us
    all_to_all x2, waiting for transfers between devices, exchange(): lax.all_to_all(values, 'dap', 0, 0, tiled=True, axis_index_groups=groups)  16.5 us
    all_to_all x2, starting transfers between devices, exchange(): lax.all_to_all(values, 'dap', 0, 0, tiled=True, axis_index_groups=groups)  16.4 us
    pallas_call x10, Pallas kernels, call(): pl.pallas_call(kernel, out_shape=out_shape, in_specs=[pl.BlockSpec(memory...  15.2 us
    all_to_all x1, blocking collectives, exchange_chips(): lax.all_to_all(values, 'dap', 0, 0, tiled=True, axis_index_groups=groups)  11.7 us
    unnamed x38, local copies, waits for them, and re-layouts  10.7 us
  transfers between devices with their start and end apart: 3, of which 3 were waited for; matrix products, arithmetic and copies ran while one was open for 0% of the time, Pallas kernels for 5%

profile of v7, /device:TPU:1, one launch (start us, length us, event | category | flops | bytes accessed | tf_op | source)
XLA Modules:
  0.0 149.3 jit_solution(6194120227612847)
XLA Ops:
  0.6 3.2 %shard_map.109 = bf16[32,64,256]{2,1,0:T(8,128)(2,1)} custom-call(bf16[8,256,128]{2,1,0:T(8,128)(2,1)} %pair_ref.1, f32[1,128]{1,0:T(1,128)} %bitcast.5, bf16[128,640]{1,0:T(8,128)(2,1)} %weight_ref.5), custom_call_target="tpu_custom_call" | custom-call | bytes 1737216 | tf_op jit(solution)/shard_map/pallas_call | solution.py:62
  3.8 11.1 %all-to-all-start = ((bf16[32,64,256]{2,1,0:T(8,128)(2,1)}), bf16[32,64,256]{2,1,0:T(8,128)(2,1)S(1)}, u32[]{:S(2)}, u32[]{:S(2)}) async-start(bf16[32,64,256]{2,1,0:T(8,128)(2,1)} %shard_map.109), calls=%async_computation | async-start | bytes 2097152 | tf_op jit(solution)/shard_map/all_to_all | solution.py:29
  15.0 0.0 copy-start.3
  15.0 1.0 copy-done.3
  16.0 0.0 copy-start.5
  16.0 1.0 copy-done.5
  17.1 0.0 copy-start.7
  17.1 0.9 copy-done.7
  18.0 0.0 copy-start.13
  18.0 0.8 copy-done.13
  18.8 0.0 copy-start.15
  18.8 0.7 copy-done.15
  19.4 0.0 copy-start.17
  19.4 0.7 copy-done.17
  20.1 3.2 %shard_map.110 = (bf16[8,128,256]{2,1,0:T(8,128)(2,1)S(1)}, f32[8,640,256]{2,1,0:T(8,128)S(1)}, bf16[8,128,256]{2,1,0:T(8,128)(2,1)S(1)}, f32[2,1024,128]{2,1,0:T(8,128)S(1)}) custom-call(bf16[8,256,128]{2,1,0:T(8,128)(2,1)S(1)} %copy-done.5, bf16[8,256,128]{2,1,0:T(8,128)(2,1)S(1)} %copy-done.3, f32[1,128]{1,0:T(1,128)S(1)} %bitcast.6, ...), custom_call_target="tpu_custom_call" | custom-call | flops 402653184 | bytes 8586240 | tf_op jit(solution)/shard_map/pallas_call | solution.py:62
  23.3 0.0 copy-start
  23.3 2.3 %copy-done = f32[8,640,256]{2,1,0:T(8,128)} copy-done((f32[8,640,256]{2,1,0:T(8,128)}, f32[8,640,256]{2,1,0:T(8,128)S(1)}, u32[]{:S(2)}) %copy-start) | copy-done | bytes 5242904
  25.7 0.0 copy-start.9
  25.7 0.8 copy-done.9
  26.5 0.0 copy-start.11
  26.5 0.0 copy-start.4
  26.5 0.0 copy-start.14
  26.5 0.0 copy-start.18
  26.5 13.6 %all-to-all-done.got_ref = bf16[32,64,256]{2,1,0:T(8,128)(2,1)S(1)} async-done(((bf16[32,64,256]{2,1,0:T(8,128)(2,1)}), bf16[32,64,256]{2,1,0:T(8,128)(2,1)S(1)}, u32[]{:S(2)}, u32[]{:S(2)}) %all-to-all-start) | async-done | bytes 1048608 | tf_op jit(solution)/shard_map/all_to_all | solution.py:29
  40.1 0.0 copy-start.1
  40.1 0.0 copy-start.10
  40.1 0.4 shard_map.111
  40.5 0.0 copy-done.11
  40.5 0.0 copy-start.12
  40.5 21.3 %all_to_all.30.got_ref.triangle_ref = bf16[32,32,256]{2,1,0:T(8,128)(2,1)S(1)} all-to-all(bf16[32,32,256]{2,1,0:T(8,128)(2,1)S(1)} %get-tuple-element.48), channel_id=1, replica_groups={{0,6,8,14,2,4,10,12,1,7,9,15,3,5,11,13,17,23,25,31,19,21,27,29,16,22,24..., dimensions={0} | all-to-all | bytes 1048576 | tf_op jit(solution)/shard_map/all_to_all | solution.py:29
  61.8 0.6 shard_map.112
  62.4 21.0 %all_to_all.31.got_ref = bf16[32,32,256]{2,1,0:T(8,128)(2,1)S(1)} all-to-all(bf16[32,32,256]{2,1,0:T(8,128)(2,1)S(1)} %shard_map.112), channel_id=1, replica_groups={{0,6,8,14,2,4,10,12,1,7,9,15,3,5,11,13,17,23,25,31,19,21,27,29,16,22,24..., dimensions={0} | all-to-all | bytes 1048576 | tf_op jit(solution)/shard_map/all_to_all | solution.py:29
  83.3 0.5 shard_map.113
  83.8 32.1 %all_to_all.32.got_ref = bf16[32,64,256]{2,1,0:T(8,128)(2,1)S(1)} all-to-all(bf16[32,64,256]{2,1,0:T(8,128)(2,1)S(1)} %shard_map.113), channel_id=1, replica_groups={{0,6,8,14,2,4,10,12,1,7,9,15,3,5,11,13,17,23,25,31,19,21,27,29,16,22,24..., dimensions={0} | all-to-all | bytes 2097152 | tf_op jit(solution)/shard_map/all_to_all | solution.py:29
  115.9 0.0 copy-done.4
  115.9 0.0 copy-done.14
  115.9 0.0 copy-done.18
  115.9 0.0 copy-done.1
  115.9 0.0 copy-done.10
  115.9 0.0 copy-done.12
  116.0 0.0 copy-start.6
  116.0 0.0 copy-start.8
  116.0 0.0 copy-start.16
  116.0 2.1 %shard_map.114 = (f32[384,128]{1,0:T(8,128)S(1)}, bf16[384,128]{1,0:T(8,128)(2,1)S(1)}) custom-call(s32[1]{0:T(128)} %bitcast.1.core_ref, bf16[32,64,256]{2,1,0:T(8,128)(2,1)S(1)} %all_to_all.32.got_ref, f32[8,640,256]{2,1,0:T(8,128)S(1)} %copy-done.1, bf16[8,128,256]{2,1,0:T(8,128)(2,1)S(1)} %copy-done.10, ...), custom_call_target="tpu_custom_call" | custom-call | bytes 8716804 | tf_op jit(solution)/shard_map/pallas_call | solution.py:62
  118.1 2.7 %collective-permute-start = (bf16[384,128]{1,0:T(8,128)(2,1)S(1)}, bf16[384,128]{1,0:T(8,128)(2,1)S(1)}, u32[]{:S(2)}, u32[]{:S(2)}) collective-permute-start(bf16[384,128]{1,0:T(8,128)(2,1)S(1)} %get-tuple-element.56), channel_id=1, source_target_pairs={{0,1},{1,0},{2,3},{3,2},{4,5},{5,4},{6,7},{7,6},{8,9},{9,8},{10,11... | collective-permute-start | bytes 294920 | tf_op jit(solution)/shard_map/ppermute | solution.py:47
  120.9 0.9 collective-permute-done.other_ref
  121.8 11.7 %all_to_all.33.got_ref = bf16[16,24,128]{2,1,0:T(8,128)(2,1)S(1)} all-to-all(bf16[16,24,128]{2,1,0:T(8,128)(2,1)S(1)} %shard_map.115), channel_id=1, replica_groups={{0,6,8,14,2,4,10,12,16,22,24,30,18,20,26,28},{1,7,9,15,3,5,11,13,17,23,..., dimensions={0} | all-to-all | bytes 196608 | tf_op jit(solution)/shard_map/all_to_all | solution.py:42
  133.5 0.7 shard_map.116
  134.2 5.3 %all-to-all-start.5 = ((bf16[32,24,128]{2,1,0:T(8,128)(2,1)}), bf16[32,24,128]{2,1,0:T(8,128)(2,1)S(1)}, u32[]{:S(2)}, u32[]{:S(2)}) async-start(bf16[32,24,128]{2,1,0:T(8,128)(2,1)} %shard_map.116), calls=%async_computation.5 | async-start | bytes 393216 | tf_op jit(solution)/shard_map/all_to_all | solution.py:29
  139.5 0.0 copy-done.6
  139.5 0.0 copy-done.8
  139.5 0.0 copy-done.16
  139.5 0.0 copy-start.2
  139.5 2.5 %copy-done.2 = f32[8,640,256]{2,1,0:T(8,128)S(1)} copy-done((f32[8,640,256]{2,1,0:T(8,128)S(1)}, f32[8,640,256]{2,1,0:T(8,128)}, u32[]{:S(2)}) %copy-start.2) | copy-done | bytes 5242904
  142.0 3.6 %shard_map.117 = (bf16[8,256,128]{2,1,0:T(8,128)(2,1)}, bf16[8,256,128]{2,1,0:T(8,128)(2,1)}) custom-call(bf16[32,64,256]{2,1,0:T(8,128)(2,1)S(1)} %all_to_all.32.got_ref, f32[8,640,256]{2,1,0:T(8,128)S(1)} %copy-done.2, bf16[8,256,128]{2,1,0:T(8,128)(2,1)S(1)} %copy-done.6, bf16[32,32,256]{2,1,0:T(8,128)(2,1)S(1)} %all_to_all.30.got_ref.triangle_ref, ...), custom_call_target="tpu_custom_call" | custom-call | flops 402653184 | bytes 9110528 | tf_op jit(solution)/shard_map/pallas_call | solution.py:62
  145.7 2.8 %all-to-all-done.5.full_ref = bf16[32,24,128]{2,1,0:T(8,128)(2,1)S(1)} async-done(((bf16[32,24,128]{2,1,0:T(8,128)(2,1)}), bf16[32,24,128]{2,1,0:T(8,128)(2,1)S(1)}, u32[]{:S(2)}, u32[]{:S(2)}) %all-to-all-start.5) | async-done | bytes 196640 | tf_op jit(solution)/shard_map/all_to_all | solution.py:29
  148.5 0.8 shard_map.118
  (1 shorter events, 0.0 us)
Async XLA Ops:
  3.8 36.3 %all-to-all-start = ((bf16[32,64,256]{2,1,0:T(8,128)(2,1)}), bf16[32,64,256]{2,1,0:T(8,128)(2,1)S(1)}, u32[]{:S(2)}, u32[]{:S(2)}) async-start(bf16[32,64,256]{2,1,0:T(8,128)(2,1)} %shard_map.109), calls=%async_computation | async-start | bytes 2097152 | tf_op jit(solution)/shard_map/all_to_all | solution.py:29
  15.0 1.0 copy-start.3
  16.0 1.0 copy-start.5
  17.1 0.9 copy-start.7
  18.0 0.8 copy-start.13
  18.8 0.7 copy-start.15
  19.4 0.7 copy-start.17
  23.3 2.3 %copy-start = (f32[8,640,256]{2,1,0:T(8,128)}, f32[8,640,256]{2,1,0:T(8,128)S(1)}, u32[]{:S(2)}) copy-start(f32[8,640,256]{2,1,0:T(8,128)S(1)} %get-tuple-element.59.factor_ref) | copy-start | bytes 15728644
  25.7 0.8 copy-start.9
  26.5 14.0 %copy-start.11 = (bf16[8,128,256]{2,1,0:T(8,128)(2,1)}, bf16[8,128,256]{2,1,0:T(8,128)(2,1)S(1)}, u32[]{:S(2)}) copy-start(bf16[8,128,256]{2,1,0:T(8,128)(2,1)S(1)} %get-tuple-element.54.grad_out_ref) | copy-start | bytes 1572868
  26.5 89.4 %copy-start.4 = (bf16[8,256,128]{2,1,0:T(8,128)(2,1)S(1)}, bf16[8,256,128]{2,1,0:T(8,128)(2,1)}, u32[]{:S(2)}) copy-start(bf16[8,256,128]{2,1,0:T(8,128)(2,1)} %cot_ref.2) | copy-start | bytes 1572868
  26.5 89.4 %copy-start.14 = (bf16[128,128]{1,0:T(8,128)(2,1)S(1)}, bf16[128,128]{1,0:T(8,128)(2,1)}, u32[]{:S(2)}) copy-start(bf16[128,128]{1,0:T(8,128)(2,1)} %w_out_ref.7) | copy-start | bytes 98308
  26.5 89.5 %copy-start.18 = (f32[128]{0:T(128)S(1)}, f32[128]{0:T(128)}, u32[]{:S(2)}) copy-start(f32[128]{0:T(128)} %param.9) | copy-start | bytes 1540
  40.1 75.8 %copy-start.1 = (f32[8,640,256]{2,1,0:T(8,128)S(1)}, f32[8,640,256]{2,1,0:T(8,128)}, u32[]{:S(2)}) copy-start(f32[8,640,256]{2,1,0:T(8,128)} %copy-done) | copy-start | bytes 15728644
  40.1 75.8 %copy-start.10 = (bf16[8,128,256]{2,1,0:T(8,128)(2,1)S(1)}, bf16[8,128,256]{2,1,0:T(8,128)(2,1)}, u32[]{:S(2)}) copy-start(bf16[8,128,256]{2,1,0:T(8,128)(2,1)} %copy-done.9) | copy-start | bytes 1572868
  40.5 75.5 %copy-start.12 = (bf16[8,128,256]{2,1,0:T(8,128)(2,1)S(1)}, bf16[8,128,256]{2,1,0:T(8,128)(2,1)}, u32[]{:S(2)}) copy-start(bf16[8,128,256]{2,1,0:T(8,128)(2,1)} %copy-done.11) | copy-start | bytes 1572868
  116.0 23.6 %copy-start.6 = (bf16[8,256,128]{2,1,0:T(8,128)(2,1)S(1)}, bf16[8,256,128]{2,1,0:T(8,128)(2,1)}, u32[]{:S(2)}) copy-start(bf16[8,256,128]{2,1,0:T(8,128)(2,1)} %pair_ref.1) | copy-start | bytes 1572868
  116.0 23.6 %copy-start.8 = (bf16[128,640]{1,0:T(8,128)(2,1)S(1)}, bf16[128,640]{1,0:T(8,128)(2,1)}, u32[]{:S(2)}) copy-start(bf16[128,640]{1,0:T(8,128)(2,1)} %weight_ref.5) | copy-start | bytes 491524
  116.0 23.6 %copy-start.16 = (f32[128]{0:T(128)S(1)}, f32[128]{0:T(128)}, u32[]{:S(2)}) copy-start(f32[128]{0:T(128)} %param.7) | copy-start | bytes 1540
  118.1 3.7 %collective-permute-start = (bf16[384,128]{1,0:T(8,128)(2,1)S(1)}, bf16[384,128]{1,0:T(8,128)(2,1)S(1)}, u32[]{:S(2)}, u32[]{:S(2)}) collective-permute-start(bf16[384,128]{1,0:T(8,128)(2,1)S(1)} %get-tuple-element.56), channel_id=1, source_target_pairs={{0,1},{1,0},{2,3},{3,2},{4,5},{5,4},{6,7},{7,6},{8,9},{9,8},{10,11... | collective-permute-start | bytes 294920 | tf_op jit(solution)/shard_map/ppermute | solution.py:47
  134.2 14.3 %all-to-all-start.5 = ((bf16[32,24,128]{2,1,0:T(8,128)(2,1)}), bf16[32,24,128]{2,1,0:T(8,128)(2,1)S(1)}, u32[]{:S(2)}, u32[]{:S(2)}) async-start(bf16[32,24,128]{2,1,0:T(8,128)(2,1)} %shard_map.116), calls=%async_computation.5 | async-start | bytes 393216 | tf_op jit(solution)/shard_map/all_to_all | solution.py:29
  139.5 2.5 %copy-start.2 = (f32[8,640,256]{2,1,0:T(8,128)S(1)}, f32[8,640,256]{2,1,0:T(8,128)}, u32[]{:S(2)}) copy-start(f32[8,640,256]{2,1,0:T(8,128)} %copy-done) | copy-start | bytes 15728644
